TPU v7x, 256 devices: a whole 4x4x8 slice. The times are simulated.
256 devices in a mesh: seq: 64 (over z, x, core), fsdp: 4 (over y).
Axes of the slice: x: 4, y: 4, z: 8, core: 2. Of those that a mesh axis runs over, the one named last changes fastest.
Arguments:
- query_rows: bfloat16 [65536, 2048], P('seq', 'fsdp'), may hold values from -5 to 5
- key_rows: bfloat16 [65536, 2048], P('seq', 'fsdp'), may hold values from -5 to 5
- value_rows: bfloat16 [65536, 2048], P('seq', 'fsdp'), may hold values from -6 to 6
- out_weight: bfloat16 [2048, 4096], P('fsdp'), may hold values from -0.125 to 0.125
- random_ids: int32 [1024, 3], P('seq'), may hold values from 0 to 1023, as said below
- global_ids: int32 [2], replicated, may hold values from 0 to 1023
Outputs:
- mixed: bfloat16 [65536, 4096], P(('seq', 'fsdp'))
Inputs may be any that keep to these rules, and one draw needn't show every extreme that they name: `random_ids`: of the 48 ids in the rows of one index of seq, at most 1 lie in the 16 blocks held by any one index of seq, and in every draw some index of seq has exactly 1 of its ids on one index of seq.
All inputs are finite; a program needn't handle non-finite values.
Results may differ from a plain program's by a relative error of at most 0.015.
Values may be sent and summed in bfloat16 or wider, within the bound.
A program may use at most 128 MiB of HBM per device.

v0:
```python
import jax
import jax.numpy as jnp
from jax import lax
from jax.sharding import PartitionSpec as P

HD = 128
BLOCK = 64
WHALF = 1
G = 2
R = 3


masked_value = -1e30


def extended(shard, sides, width):
    for axis, dim in sides:
        count, length = (lax.axis_size(axis), shard.shape[dim])
        up = [(i, (i + 1) % count) for i in range(count - 1)]
        down = [(j, i) for i, j in up]
        last = lax.slice_in_dim(shard, length - width, length, axis=dim)
        first = lax.slice_in_dim(shard, 0, width, axis=dim)
        before = lax.ppermute(last, axis, up)
        after = lax.ppermute(first, axis, down)
        shard = jnp.concatenate([before, shard, after], axis=dim)
    return shard


def on_device(query_rows, key_rows, value_rows, out_weight, random_ids, global_ids):
    tokens_here, width_dev = query_rows.shape
    head_size = HD
    heads_dev = width_dev // head_size
    seq_devices = lax.axis_size("seq")
    blocks_dev = tokens_here // BLOCK
    total_blocks = blocks_dev * seq_devices
    position = lax.axis_index("seq")
    count_keys = 2 * WHALF + 1 + G + R
    key_value = jnp.concatenate([key_rows, value_rows], axis=1)
    pair_blocks = key_value.reshape(blocks_dev, BLOCK, 2 * width_dev)
    rim_rows = WHALF * BLOCK
    padded = extended(key_value, (("seq", 0),), rim_rows)
    padded_blocks = padded.reshape(blocks_dev + 2 * WHALF, BLOCK, 2 * width_dev)
    window_blocks = jnp.stack(
        [padded_blocks[offset : offset + blocks_dev] for offset in range(2 * WHALF + 1)], axis=1
    )
    owners = global_ids // blocks_dev
    spot_index = global_ids % blocks_dev
    picked = pair_blocks[spot_index]
    is_owner = (owners == position)[:, None, None]
    global_share = jnp.where(is_owner, picked.astype(jnp.float32), 0.0)
    global_pair = lax.psum(global_share, "seq").astype(jnp.bfloat16)
    request_count = random_ids.shape[0] * random_ids.shape[1]
    slot_cap = (request_count + seq_devices - 1) // seq_devices
    flat_ids = random_ids.reshape(request_count)
    id_owners = flat_ids // blocks_dev
    id_spots = flat_ids % blocks_dev
    positions = jnp.arange(request_count)
    same_owner = (id_owners[:, None] == id_owners[None, :]) & (
        positions[None, :] < positions[:, None]
    )
    slot_rank = jnp.sum(same_owner.astype(jnp.int32), axis=1)
    slot_index = id_owners * slot_cap + slot_rank
    slot_hits = slot_index[:, None] == jnp.arange(seq_devices * slot_cap)[None, :]
    request_table = jnp.sum(jnp.where(slot_hits, id_spots[:, None], 0), axis=0)
    request_table = request_table.reshape(seq_devices, slot_cap)
    served = pair_blocks[
        lax.all_to_all(request_table, "seq", split_axis=0, concat_axis=0, tiled=True)
    ]
    fetched = lax.all_to_all(served, "seq", split_axis=0, concat_axis=0, tiled=True)
    fetched = fetched.reshape(seq_devices * slot_cap, BLOCK, 2 * width_dev)
    remote = fetched[slot_index].reshape(blocks_dev, R, BLOCK, 2 * width_dev)
    global_wide = jnp.broadcast_to(global_pair[None], (blocks_dev, G, BLOCK, 2 * width_dev))
    assembled = jnp.concatenate([window_blocks, global_wide, remote], axis=1)
    assembled = assembled.reshape(blocks_dev, count_keys * BLOCK, 2 * width_dev)
    key_part = assembled[:, :, :width_dev].reshape(
        blocks_dev, count_keys * BLOCK, heads_dev, head_size
    )
    value_part = assembled[:, :, width_dev:].reshape(
        blocks_dev, count_keys * BLOCK, heads_dev, head_size
    )
    block_ids = position * blocks_dev + jnp.arange(blocks_dev, dtype=jnp.int32)
    offsets = jnp.arange(-WHALF, WHALF + 1, dtype=jnp.int32)
    near_ids = block_ids[:, None] + offsets[None, :]
    inside = (near_ids >= 0) & (near_ids < total_blocks)
    key_valid = jnp.concatenate([inside, jnp.ones((blocks_dev, G + R), dtype=bool)], axis=1)
    key_mask = jnp.repeat(key_valid, BLOCK, axis=1)[:, None, None, :]
    query_blocks = query_rows.reshape(blocks_dev, BLOCK, heads_dev, head_size)
    score_scale = head_size ** (-0.5)
    scores = (
        jnp.einsum("qbhd,qkhd->qhbk", query_blocks, key_part, preferred_element_type=jnp.float32)
        * score_scale
    )
    scores = jnp.where(key_mask, scores, masked_value)
    row_max = jnp.max(scores, axis=-1, keepdims=True)
    lifted = jnp.exp(scores - row_max)
    attn_weights = (lifted / jnp.sum(lifted, axis=-1, keepdims=True)).astype(jnp.bfloat16)
    context = jnp.einsum(
        "qhbk,qkhd->qbhd", attn_weights, value_part, preferred_element_type=jnp.float32
    )
    context = context.astype(jnp.bfloat16).reshape(tokens_here, width_dev)
    all_heads = lax.all_to_all(context, "fsdp", split_axis=0, concat_axis=1, tiled=True)
    summed = jnp.dot(
        all_heads,
        lax.all_gather(out_weight, "fsdp", axis=0, tiled=True),
        preferred_element_type=jnp.float32,
    )
    return summed.astype(jnp.bfloat16)


def solution(mesh):
    return jax.shard_map(
        on_device,
        mesh=mesh,
        in_specs=(
            P("seq", "fsdp"),
            P("seq", "fsdp"),
            P("seq", "fsdp"),
            P("fsdp", None),
            P("seq", None),
            P(),
        ),
        out_specs=P(("seq", "fsdp"), None),
        check_vma=False,
    )
```

profile of v0, /device:TPU:102, one launch (start us, length us, event | category | flops | bytes accessed | tf_op | source)
XLA Modules:
  0.0 584.8 jit_solution(15963489200330119033)
XLA Ops:
  6.5 0.0 all-gather.2.cloned.1.call-start
  6.5 0.7 all-gather.2.cloned.1.call-update
  7.3 0.8 copy.63
  8.0 0.1 reshape.220
  8.1 0.2 convert_reduce_fusion
  8.3 0.1 select_reduce_fusion
  8.4 0.7 copy.64
  9.1 10.7 %all-to-all-start = ((s32[64,1,1]{2,1,0:T(1,128)}), s32[64,1,1]{2,1,0:T(1,128)S(1)}, u32[]{:S(2)}, u32[]{:S(2)}) async-start(s32[64,1,1]{2,1,0:T(1,128)} %copy.64), calls=%async_computation | async-start | bytes 65536 | tf_op jit(solution)/shard_map/all_to_all | solution.py:67
  19.8 1.4 constant_dynamic-update-slice_fusion.1
  21.2 0.7 compare_select_fusion.2
  21.9 1.5 constant_dynamic-update-slice_fusion
  23.4 1.7 all-to-all-done
  25.1 1.2 fusion.13
  26.4 5.6 gather_fusion.1
  31.9 0.0 copy-start
  31.9 9.9 %all-to-all-start.1 = ((bf16[64,1,64,1024]{3,2,1,0:T(8,128)(2,1)}), bf16[64,1,64,1024]{3,2,1,0:T(8,128)(2,1)}, u32[]{:S(2)}, u32[]{:S(2)}) async-start(bf16[64,1,64,1024]{3,2,1,0:T(8,128)(2,1)} %bitcast.40), calls=%async_computation.1 | async-start | bytes 16777216 | tf_op jit(solution)/shard_map/all_to_all | solution.py:69
  41.8 0.7 fusion.21
  42.5 2.0 collective-permute-start
  44.6 3.5 collective-permute-start.1
  48.1 0.1 reshape.222
  48.2 1.4 reshape.227
  49.6 0.1 fusion.15
  49.7 0.1 copy.76
  49.8 0.1 broadcast_in_dim.71
  49.9 0.1 broadcast_in_dim.72
  50.0 0.0 copy-done
  50.0 0.5 fusion.17
  50.6 0.6 gather_fusion
  51.1 1.5 convert_select_fusion
  52.7 414.1 %all-reduce.2 = bf16[2,64,1024]{2,1,0:T(8,128)(2,1)S(1)} all-reduce(f32[2,64,1024]{2,1,0:T(8,128)} %convert_select_fusion), channel_id=1, replica_groups=mesh['seq'=64,'fsdp'=4] {'seq'}, use_global_device_ids=true, to_apply=%region_0.1 | all-reduce | flops 131072 | bytes 786432 | tf_op jit(solution)/shard_map/psum | solution.py:51
  466.8 0.0 collective-permute-done
  466.8 0.0 collective-permute-done.1
  466.8 1.4 pad_maximum_fusion
  468.2 1.4 constant_dynamic-update-slice_fusion.5
  469.7 1.6 constant_dynamic-update-slice_fusion.4
  471.2 1.4 constant_dynamic-update-slice_fusion.3
  472.7 2.5 broadcast_dynamic-update-slice_fusion
  475.1 0.0 all-to-all-done.1
  475.1 8.4 %gather_fusion.2 = bf16[48,64,1024]{2,1,0:T(8,128)(2,1)} fusion(bf16[64,64,1024]{2,1,0:T(8,128)(2,1)} %bitcast.6, s32[1024]{0:T(1024)S(1)} %pad_clamp_fusion), kind=kCustom, calls=%fused_computation.2 | custom fusion | bytes 12583104 | tf_op jit(solution)/shard_map/gather | solution.py:71
  483.5 6.6 %constant_dynamic-update-slice_fusion.2 = bf16[16,8,64,1024]{3,2,1,0:T(8,128)(2,1)} fusion(bf16[16,8,64,1024]{3,2,1,0:T(8,128)(2,1)} %broadcast_dynamic-update-slice_fusion, bf16[16,3,64,1024]{3,2,1,0:T(8,128)(2,1)} %bitcast.41), kind=kLoop, calls=%fused_computation.32 | loop fusion | bytes 12582912 | tf_op jit(solution)/shard_map/concatenate | solution.py:73
  490.1 11.3 %fusion.20 = (bf16[16,512,512]{2,1,0:T(8,128)(2,1)}, bf16[16,512,512]{2,1,0:T(8,128)(2,1)}) fusion(bf16[16,512,1024]{2,1,0:T(8,128)(2,1)} %bitcast.10), kind=kLoop, calls=%fused_computation.65 | loop fusion | bytes 33554432 | tf_op jit(solution)/shard_map/slice | solution.py:75
  501.4 12.3 %copy.68 = bf16[16,512,512]{1,2,0:T(8,128)(2,1)} copy(bf16[16,512,512]{2,1,0:T(8,128)(2,1)} %get-tuple-element.5) | data formatting | bytes 16777216 | tf_op jit(solution)/shard_map/slice | solution.py:75
  513.7 12.3 %copy.66 = bf16[16,512,512]{1,2,0:T(8,128)(2,1)} copy(bf16[16,512,512]{2,1,0:T(8,128)(2,1)} %get-tuple-element.6) | data formatting | bytes 16777216 | tf_op jit(solution)/shard_map/slice | solution.py:78
  526.1 4.6 fusion.11
  530.7 4.8 fusion.22
  535.5 8.8 %fusion.10 = bf16[16,64,4,128]{3,1,2,0:T(8,128)(2,1)S(1)} fusion(bf16[16,512,4,128]{1,3,2,0:T(8,128)(2,1)} %bitcast.44, f32[16,4,64,512]{3,2,1,0:T(8,128)} %get-tuple-element.14, f32[16,4,64]{2,1,0:T(4,128)S(1)} %get-tuple-element.13), kind=kOutput, calls=%fused_computation.19 | convolution fusion | flops 541589504 | bytes 17842176 | tf_op jit(solution)/shard_map/qhbk,qkhd->qbhd/dot_general | solution.py:97
  544.4 0.9 copy.72
  545.3 0.4 all_to_all.26
  545.7 20.2 %all_to_all.33 = bf16[4,256,512]{2,1,0:T(8,128)(2,1)S(1)} all-to-all(bf16[4,256,512]{2,1,0:T(8,128)(2,1)S(1)} %all_to_all.26), channel_id=1, replica_groups=mesh['seq'=64,'fsdp'=4] {'fsdp'}, dimensions={0} | all-to-all | bytes 2097152 | tf_op jit(solution)/shard_map/all_to_all | solution.py:101
  565.9 0.5 copy.73
  566.4 0.0 all-gather.2.cloned.1.call-done
  566.5 11.5 %convolution_convert_fusion = bf16[256,4096]{1,0:T(8,128)(2,1)} fusion(bf16[256,2048]{0,1:T(8,128)(2,1)S(1)} %bitcast.45, bf16[2048,4096]{1,0:T(8,128)(2,1)} %all-gather.2.cloned.1.call-done), kind=kOutput, calls=%fused_computation.10 | convolution fusion | flops 4296015872 | bytes 19922944 | tf_op jit(solution)/shard_map/dot_general | solution.py:102
  (8 shorter events, 0.1 us)
Async XLA Ops:
  6.5 559.9 %all-gather.2.cloned.1.call-start = ((), (), s32[]{:S(2)}) async-start(), calls=%async_computation.3 | async-start | bytes 20971520 | tf_op jit(solution)/shard_map/all_gather | solution.py:104
  9.1 16.0 %all-to-all-start = ((s32[64,1,1]{2,1,0:T(1,128)}), s32[64,1,1]{2,1,0:T(1,128)S(1)}, u32[]{:S(2)}, u32[]{:S(2)}) async-start(s32[64,1,1]{2,1,0:T(1,128)} %copy.64), calls=%async_computation | async-start | bytes 65536 | tf_op jit(solution)/shard_map/all_to_all | solution.py:67
  31.9 18.1 %copy-start = (s32[2]{0:T(128)S(1)}, s32[2]{0:T(128)}, u32[]{:S(2)}) copy-start(s32[2]{0:T(128)} %param.11) | copy-start | bytes 28
  31.9 443.2 %all-to-all-start.1 = ((bf16[64,1,64,1024]{3,2,1,0:T(8,128)(2,1)}), bf16[64,1,64,1024]{3,2,1,0:T(8,128)(2,1)}, u32[]{:S(2)}, u32[]{:S(2)}) async-start(bf16[64,1,64,1024]{3,2,1,0:T(8,128)(2,1)} %bitcast.40), calls=%async_computation.1 | async-start | bytes 16777216 | tf_op jit(solution)/shard_map/all_to_all | solution.py:69
  42.5 424.3 %collective-permute-start = (bf16[64,1024]{1,0:T(8,128)(2,1)}, bf16[64,1024]{1,0:T(8,128)(2,1)S(1)}, u32[]{:S(2)}, u32[]{:S(2)}) collective-permute-start(bf16[64,1024]{1,0:T(8,128)(2,1)} %get-tuple-element.10), channel_id=1, source_target_pairs={{0,4},{4,8},{8,12},{12,16},{16,20},{20,24},{24,28},{28,32},{32,36}... | collective-permute-start | bytes 393224 | tf_op jit(solution)/shard_map/ppermute | solution.py:23
  44.6 422.2 %collective-permute-start.1 = (bf16[64,1024]{1,0:T(8,128)(2,1)}, bf16[64,1024]{1,0:T(8,128)(2,1)}, u32[]{:S(2)}, u32[]{:S(2)}) collective-permute-start(bf16[64,1024]{1,0:T(8,128)(2,1)} %get-tuple-element.9), channel_id=1, source_target_pairs={{4,0},{8,4},{12,8},{16,12},{20,16},{24,20},{28,24},{32,28},{36,32}... | collective-permute-start | bytes 393224 | tf_op jit(solution)/shard_map/ppermute | solution.py:24
Sparse Core Ops, SparseCore 0:
  9.2 158.4 all-gather.1
where the time goes:
time: 586 us; the launch traced here: 585 us
  blocking collectives  434 us (74%)
  local copies, waits for them, and re-layouts  72.7 us (12%)
  starting transfers between devices  26.1 us (4%)
  matrix products  25 us (4%)
  between operations  13.6 us (2%)
  other arithmetic  10.6 us (2%)
    psum x1, blocking collectives, on_device(): global_pair = lax.psum(global_share, 'seq').astype(jnp.bfloat16)  414 us
    slice x2, local copies, waits for them, and re-layouts, on_device(): assembled[:, :, :width_dev]  23.6 us
    all_to_all x1, blocking collectives, on_device(): lax.all_to_all(context, 'fsdp', split_axis=0, concat_axis=1, tiled=True)  20.2 us
    slice x1, local copies, waits for them, and re-layouts, on_device(): assembled[:, :, width_dev:]  12.3 us
  transfers between devices with their start and end apart: 5, of which 1 were waited for; matrix products, arithmetic and copies ran while one was open for 16% of the time, Pallas kernels for 0%

commit v1 on v0

v1 whole, which is shorter than its diff:
```python
import functools

import jax
import jax.numpy as jnp
from jax import lax
from jax.experimental import pallas as pl
from jax.experimental.pallas import tpu as pltpu
from jax.sharding import PartitionSpec as P

HD = 128
BLOCK = 64
G = 2
R = 3
LOW = -1e30
NT = (((1,), (1,)), ((), ()))


def near_kernel(edge_ref, q_ref, k_ref, v_ref, g_ref, acc_ref, max_ref, sum_ref):
    step = pl.program_id(0)
    heads = q_ref.shape[1] // HD
    width = q_ref.shape[1]
    rows = q_ref.shape[0]
    span = rows + 2 * BLOCK
    count = span + G * BLOCK
    row_block = lax.broadcasted_iota(jnp.int32, (rows, count), 0) // BLOCK
    column = lax.broadcasted_iota(jnp.int32, (rows, count), 1)
    key_block = column // BLOCK
    first = edge_ref[0] * jnp.where(step == 0, 1, 0)
    last = edge_ref[1] * jnp.where(step == pl.num_programs(0) - 1, 1, 0)
    near = (key_block >= row_block) & (key_block <= row_block + 2)
    near = near & (key_block >= first) & (key_block < span // BLOCK - last)
    listed = near | (column >= span)
    here = pl.ds(pl.multiple_of(step * rows, rows), span)
    for head in range(heads):
        cols = slice(head * HD, (head + 1) * HD)
        value_cols = slice(width + head * HD, width + (head + 1) * HD)
        keys = jnp.concatenate([k_ref[here, cols], g_ref[:, cols]], axis=0)
        values = jnp.concatenate([v_ref[here, cols], g_ref[:, value_cols]], axis=0)
        scores = lax.dot_general(q_ref[:, cols], keys, NT, preferred_element_type=jnp.float32)
        scores = jnp.where(listed, scores * HD**-0.5, LOW)
        row_max = jnp.max(scores, axis=1, keepdims=True)
        lifted = jnp.exp(scores - row_max)
        row_sum = jnp.sum(lifted, axis=1, keepdims=True)
        acc_ref[:, cols] = jnp.dot(lifted.astype(jnp.bfloat16), values, preferred_element_type=jnp.float32)
        max_ref[:, cols] = jnp.broadcast_to(row_max, (rows, HD))
        sum_ref[:, cols] = jnp.broadcast_to(row_sum, (rows, HD))


def near_part(edges, query, key_pad, value_pad, shared):
    tokens, width = query.shape
    rows = 2 * BLOCK
    whole = lambda array: pl.BlockSpec(array.shape, lambda i, e: (0, 0))
    tile = pl.BlockSpec((rows, width), lambda i, e: (i, 0))
    out = jax.ShapeDtypeStruct((tokens, width), jnp.float32)
    return pl.pallas_call(
        near_kernel,
        grid_spec=pltpu.PrefetchScalarGridSpec(
            num_scalar_prefetch=1,
            grid=(tokens // rows,),
            in_specs=[tile, whole(key_pad), whole(value_pad), whole(shared)],
            out_specs=[tile, tile, tile],
        ),
        out_shape=[out, out, out],
        cost_estimate=pl.CostEstimate(flops=2 * 10**9, bytes_accessed=12 * 10**6, transcendentals=2 * 10**6),
        compiler_params=pltpu.CompilerParams(vmem_limit_bytes=30 << 20),
    )(edges, query, key_pad, value_pad, shared)


def far_kernel(slot_ref, q_ref, acc_ref, max_ref, sum_ref, *rest):
    blocks, out_ref = rest[:-1], rest[-1]
    width = q_ref.shape[1]
    per = q_ref.shape[0] // BLOCK
    for b in range(per):
        rows = slice(b * BLOCK, (b + 1) * BLOCK)
        mine = blocks[b * R : (b + 1) * R]
        for head in range(width // HD):
            cols = slice(head * HD, (head + 1) * HD)
            value_cols = slice(width + head * HD, width + (head + 1) * HD)
            keys = jnp.concatenate([block[0, :, cols] for block in mine], axis=0)
            values = jnp.concatenate([block[0, :, value_cols] for block in mine], axis=0)
            scores = lax.dot_general(q_ref[rows, cols], keys, NT, preferred_element_type=jnp.float32)
            scores = scores * HD**-0.5
            near_max = max_ref[rows, cols]
            row_max = jnp.maximum(jnp.max(scores, axis=1, keepdims=True), near_max)
            lifted = jnp.exp(scores - row_max[:, :1])
            scale = jnp.exp(near_max - row_max)
            row_sum = scale * sum_ref[rows, cols] + jnp.sum(lifted, axis=1, keepdims=True)
            total = scale * acc_ref[rows, cols] + jnp.dot(
                lifted.astype(jnp.bfloat16), values, preferred_element_type=jnp.float32
            )
            out_ref[rows, cols] = (total / row_sum).astype(jnp.bfloat16)


def far_part(slots, query, acc, near_max, near_sum, fetched):
    tokens, width = query.shape
    per = 2
    rows = per * BLOCK
    tile = pl.BlockSpec((rows, width), lambda i, s: (i, 0))

    def pick(j):
        return pl.BlockSpec((1, BLOCK, 2 * width), lambda i, s: (s[i * per * R + j], 0, 0))

    return pl.pallas_call(
        far_kernel,
        grid_spec=pltpu.PrefetchScalarGridSpec(
            num_scalar_prefetch=1,
            grid=(tokens // rows,),
            in_specs=[tile] * 4 + [pick(j) for j in range(per * R)],
            out_specs=tile,
        ),
        out_shape=jax.ShapeDtypeStruct((tokens, width), jnp.bfloat16),
        cost_estimate=pl.CostEstimate(flops=10**9, bytes_accessed=15 * 10**6, transcendentals=10**6),
        compiler_params=pltpu.CompilerParams(vmem_limit_bytes=30 << 20),
    )(slots, query, acc, near_max, near_sum, *([fetched] * (per * R)))


def on_device(query_rows, key_rows, value_rows, out_weight, random_ids, global_ids):
    tokens, width = query_rows.shape
    n = lax.axis_size("seq")
    blocks = tokens // BLOCK
    me = lax.axis_index("seq")
    flat = random_ids.reshape(-1)
    owners, spots = flat // blocks, flat % blocks
    hits = owners[:, None] == jnp.arange(n)[None, :]
    table = jnp.sum(jnp.where(hits, spots[:, None], 0), axis=0)
    wanted = lax.all_to_all(table, "seq", split_axis=0, concat_axis=0, tiled=True)
    pair = jnp.concatenate([key_rows, value_rows], axis=1)
    pair_blocks = pair.reshape(blocks, BLOCK, 2 * width)
    picked = pair_blocks[global_ids % blocks]
    pieces = picked.transpose(1, 0, 2)
    pieces = lax.all_to_all(pieces, "seq", split_axis=0, concat_axis=0, tiled=True)
    piece = pieces[global_ids // blocks, jnp.arange(G)]
    shared = lax.all_gather(piece, "seq", axis=1, tiled=False).reshape(G * BLOCK, 2 * width)
    served = pair_blocks[wanted]
    fetched = lax.all_to_all(served, "seq", split_axis=0, concat_axis=0, tiled=True)
    up = [(i, i + 1) for i in range(n - 1)]
    down = [(j, i) for i, j in up]
    before = lax.ppermute(pair[-BLOCK:], "seq", up)
    after = lax.ppermute(pair[:BLOCK], "seq", down)
    padded = jnp.concatenate([before, pair, after], axis=0)
    edges = jnp.stack([me == 0, me == n - 1]).astype(jnp.int32)
    acc, near_max, near_sum = near_part(edges, query_rows, padded[:, :width], padded[:, width:], shared)
    context = far_part(owners, query_rows, acc, near_max, near_sum, fetched)
    all_heads = lax.all_to_all(context, "fsdp", split_axis=0, concat_axis=1, tiled=True)
    weight = lax.all_gather(out_weight, "fsdp", axis=0, tiled=True)
    return jnp.dot(all_heads, weight, preferred_element_type=jnp.float32).astype(jnp.bfloat16)


def solution(mesh):
    return jax.shard_map(
        on_device,
        mesh=mesh,
        in_specs=(
            P("seq", "fsdp"),
            P("seq", "fsdp"),
            P("seq", "fsdp"),
            P("fsdp", None),
            P("seq", None),
            P(),
        ),
        out_specs=P(("seq", "fsdp"), None),
        check_vma=False,
    )
```

time: 586 us -> 375 us (0.64)
  the two profiles are of different devices: /device:TPU:102 before, /device:TPU:1 now
where the time goes in v1:
time: 375 us; the launch traced here: 374 us
  blocking collectives  217 us (58%)
  waiting for transfers between devices  43 us (11%)
  Pallas kernels  36.8 us (10%)
  starting transfers between devices  28.6 us (8%)
  local copies, waits for them, and re-layouts  21.6 us (6%)
  between operations  13.6 us (4%)
  matrix products  11.5 us (3%)
    all_gather x1, blocking collectives, on_device(): lax.all_gather(piece, 'seq', axis=1, tiled=False)  198 us
    pallas_call x1, Pallas kernels, far_part(): pl.pallas_call(far_kernel, grid_spec=pltpu.PrefetchScalarGridSpec(num_sca...  26.8 us
    all_to_all x1, blocking collectives, on_device(): lax.all_to_all(context, 'fsdp', split_axis=0, concat_axis=1, tiled=True)  18.7 us
    ppermute x1, waiting for transfers between devices, on_device(): before = lax.ppermute(pair[-BLOCK:], 'seq', up)  17.3 us
    all_to_all x1, starting transfers between devices, on_device(): lax.all_to_all(table, 'seq', split_axis=0, concat_axis=0, tiled=True)  13 us
    dot_general x1, matrix products, on_device(): jnp.dot(all_heads, weight, preferred_element_type=jnp.float32)  11.5 us
    unnamed x26, local copies, waits for them, and re-layouts  10.8 us
    pallas_call x1, Pallas kernels, near_part(): pl.pallas_call(near_kernel, grid_spec=pltpu.PrefetchScalarGridSpec(num_sc...  10 us
  transfers between devices with their start and end apart: 6, of which 4 were waited for; matrix products, arithmetic and copies ran while one was open for 3% of the time, Pallas kernels for 10%

profile of v1, /device:TPU:1, one launch (start us, length us, event | category | flops | bytes accessed | tf_op | source)
XLA Modules:
  0.0 374.0 jit_solution(14350237163904621553)
XLA Ops:
  6.5 0.0 copy-start.10
  6.5 0.0 copy-start.8
  6.5 0.0 copy-start.11
  6.5 0.0 all-gather.3.cloned.1.call-start
  6.5 0.7 all-gather.3.cloned.1.call-update
  7.3 0.0 copy-done.10
  7.3 0.1 copy.19
  7.4 0.1 reshape.91
  7.5 0.1 select_reduce_fusion
  7.6 0.7 copy.21
  8.3 13.0 %all-to-all-start.1 = ((s32[64,1,1]{2,1,0:T(1,128)}), s32[64,1,1]{2,1,0:T(1,128)S(1)}, u32[]{:S(2)}, u32[]{:S(2)}) async-start(s32[64,1,1]{2,1,0:T(1,128)} %copy.21), calls=%async_computation.1 | async-start | bytes 65536 | tf_op jit(solution)/shard_map/all_to_all | solution.py:126
  21.3 0.0 copy-done.8
  21.3 0.0 copy-start.9
  21.3 0.1 constant_dynamic-update-slice_fusion.1
  21.5 0.0 copy-done.11
  21.5 1.0 copy-done.9
  22.5 0.1 constant_dynamic-update-slice_fusion
  22.7 7.9 %all-to-all-done.1 = s32[64,1,1]{2,1,0:T(1,128)S(1)} async-done(((s32[64,1,1]{2,1,0:T(1,128)}), s32[64,1,1]{2,1,0:T(1,128)S(1)}, u32[]{:S(2)}, u32[]{:S(2)}) %all-to-all-start.1) | async-done | bytes 288 | tf_op jit(solution)/shard_map/all_to_all | solution.py:126
  30.6 1.2 reduce
  31.8 0.6 gather_fusion
  32.4 1.0 copy.20
  33.4 4.7 %all-to-all-start = ((bf16[64,2,1024]{2,1,0:T(2,128)(2,1)}), bf16[64,2,1024]{2,1,0:T(2,128)(2,1)S(1)}, u32[]{:S(2)}, u32[]{:S(2)}) async-start(bf16[64,2,1024]{2,1,0:T(2,128)(2,1)} %copy.20), calls=%async_computation | async-start | bytes 524288 | tf_op jit(solution)/shard_map/all_to_all | solution.py:131
  38.1 5.3 %gather_fusion.2 = bf16[64,64,1024]{2,1,0:T(8,128)(2,1)} fusion(bf16[16,64,1024]{2,1,0:T(8,128)(2,1)S(1)} %bitcast.25, s32[1024]{0:T(1024)S(1)} %get-tuple-element.17), kind=kCustom, calls=%fused_computation.2 | custom fusion | bytes 16777472 | tf_op jit(solution)/shard_map/gather | solution.py:134
  43.5 7.9 %all-to-all-done = bf16[64,2,1024]{2,1,0:T(2,128)(2,1)S(1)} async-done(((bf16[64,2,1024]{2,1,0:T(2,128)(2,1)}), bf16[64,2,1024]{2,1,0:T(2,128)(2,1)S(1)}, u32[]{:S(2)}, u32[]{:S(2)}) %all-to-all-start) | async-done | bytes 262176 | tf_op jit(solution)/shard_map/all_to_all | solution.py:131
  51.4 5.4 %all-to-all-start.2 = ((bf16[64,64,1024]{2,1,0:T(8,128)(2,1)}), bf16[64,64,1024]{2,1,0:T(8,128)(2,1)}, u32[]{:S(2)}, u32[]{:S(2)}) async-start(bf16[64,64,1024]{2,1,0:T(8,128)(2,1)} %gather_fusion.2), calls=%async_computation.2 | async-start | bytes 16777216 | tf_op jit(solution)/shard_map/all_to_all | solution.py:135
  56.8 3.5 collective-permute-start
  60.4 1.9 collective-permute-start.1
  62.3 0.1 add_convert_fusion.edge_ref
  62.4 17.3 %collective-permute-done = bf16[64,1024]{1,0:T(8,128)(2,1)S(1)} collective-permute-done((bf16[64,1024]{1,0:T(8,128)(2,1)S(1)}, bf16[64,1024]{1,0:T(8,128)(2,1)S(1)}, u32[]{:S(2)}, u32[]{:S(2)}) %collective-permute-start) | collective-permute-done | bytes 131104 | tf_op jit(solution)/shard_map/ppermute | solution.py:138
  79.7 9.2 %collective-permute-done.1 = bf16[64,1024]{1,0:T(8,128)(2,1)S(1)} collective-permute-done((bf16[64,1024]{1,0:T(8,128)(2,1)S(1)}, bf16[64,1024]{1,0:T(8,128)(2,1)S(1)}, u32[]{:S(2)}, u32[]{:S(2)}) %collective-permute-start.1) | collective-permute-done | bytes 131104 | tf_op jit(solution)/shard_map/ppermute | solution.py:139
  88.9 0.2 pad_maximum_fusion
  89.1 0.0 copy-start.6
  89.1 1.6 fusion.6
  90.7 0.6 gather_fusion.1
  91.3 198.5 %all-gather = bf16[2,65536]{1,0:T(2,128)(2,1)S(1)} all-gather(bf16[2,1024]{1,0:T(2,128)(2,1)S(1)} %gather_fusion.1), channel_id=2, replica_groups=mesh['seq'=64,'fsdp'=4] {'seq'}, dimensions={1}, use_global_device_ids=true | all-gather | bytes 266240 | tf_op jit(solution)/shard_map/all_gather | solution.py:133
  289.8 0.2 reshape.93.g_ref
  290.0 0.0 copy-done.6
  290.0 0.0 copy-start.4
  290.0 1.3 copy-done.4
  291.3 0.0 copy-start.5
  291.3 1.3 copy-done.5
  292.5 10.0 %shard_map.64 = (f32[1024,512]{1,0:T(8,128)S(1)}, f32[1024,512]{1,0:T(8,128)S(1)}, f32[1024,512]{1,0:T(8,128)S(1)}) custom-call(s32[2]{0:T(128)S(1)} %add_convert_fusion.edge_ref, bf16[1024,512]{1,0:T(8,128)(2,1)S(1)} %copy-done.6, bf16[1152,512]{1,0:T(8,128)(2,1)S(1)} %copy-done.5, bf16[1152,512]{1,0:T(8,128)(2,1)S(1)} %copy-done.4, ...), custom_call_target="tpu_custom_call" | custom-call | flops 2000000000 | bytes 12000000 | tf_op jit(solution)/shard_map/pallas_call | solution.py:55
  302.5 0.0 copy-start
  302.6 1.3 copy-done
  303.9 0.0 copy-start.2
  303.9 1.3 copy-done.2
  305.2 0.0 all-to-all-done.2.rest_0_.rest_1_.rest_2_.rest_3_.rest_4_.rest_5_
  305.2 0.0 copy-start.1
  305.2 1.6 copy-done.1
  306.8 0.0 copy-start.3
  306.8 1.6 copy-done.3
  308.3 0.0 copy-start.7
  308.4 1.2 copy-done.7
  309.6 26.8 %shard_map.65 = bf16[1024,512]{1,0:T(8,128)(2,1)S(1)} custom-call(s32[48]{0:T(128)S(1)} %get-tuple-element.16.slot_ref, bf16[1024,512]{1,0:T(8,128)(2,1)S(1)} %copy-done.7, f32[1024,512]{1,0:T(8,128)S(1)} %get-tuple-element.8.acc_ref, f32[1024,512]{1,0:T(8,128)S(1)} %copy-done.1, f32[1024,512]{1,0:T(8,128)S(1)} %copy-done.3, ...), custom_call_target="tpu_custom_call" | custom-call | flops 1000000000 | bytes 15000000 | tf_op jit(solution)/shard_map/pallas_call | solution.py:103
  336.4 0.5 copy.22
  336.9 18.7 %all_to_all.41 = bf16[4,256,512]{1,2,0:T(8,128)(2,1)S(1)} all-to-all(bf16[4,256,512]{1,2,0:T(8,128)(2,1)S(1)} %copy.22), channel_id=1, replica_groups=mesh['seq'=64,'fsdp'=4] {'fsdp'}, dimensions={0} | all-to-all | bytes 2097152 | tf_op jit(solution)/shard_map/all_to_all | solution.py:144
  355.6 0.0 all-gather.3.cloned.1.call-done
  355.6 11.5 %convolution_convert_fusion = bf16[256,4096]{1,0:T(8,128)(2,1)} fusion(bf16[256,2048]{0,1:T(8,128)(2,1)S(1)} %bitcast.26, bf16[2048,4096]{1,0:T(8,128)(2,1)} %all-gather.3.cloned.1.call-done), kind=kOutput, calls=%fused_computation.3 | convolution fusion | flops 4296015872 | bytes 19922944 | tf_op jit(solution)/shard_map/dot_general | solution.py:146
  (6 shorter events, 0.1 us)
Async XLA Ops:
  6.5 0.7 copy-start.10
  6.5 14.8 %copy-start.8 = (bf16[1024,512]{1,0:T(8,128)(2,1)S(1)}, bf16[1024,512]{1,0:T(8,128)(2,1)}, u32[]{:S(2)}) copy-start(bf16[1024,512]{1,0:T(8,128)(2,1)} %param.7) | copy-start | bytes 3145732
  6.5 14.9 %copy-start.11 = (s32[2]{0:T(128)S(1)}, s32[2]{0:T(128)}, u32[]{:S(2)}) copy-start(s32[2]{0:T(128)} %param.11) | copy-start | bytes 28
  6.5 349.1 %all-gather.3.cloned.1.call-start = ((), (), s32[]{:S(2)}) async-start(), calls=%async_computation.4 | async-start | bytes 20971520 | tf_op jit(solution)/shard_map/all_gather | solution.py:145
  8.3 22.3 %all-to-all-start.1 = ((s32[64,1,1]{2,1,0:T(1,128)}), s32[64,1,1]{2,1,0:T(1,128)S(1)}, u32[]{:S(2)}, u32[]{:S(2)}) async-start(s32[64,1,1]{2,1,0:T(1,128)} %copy.21), calls=%async_computation.1 | async-start | bytes 65536 | tf_op jit(solution)/shard_map/all_to_all | solution.py:126
  21.3 1.2 copy-start.9
  33.4 18.0 %all-to-all-start = ((bf16[64,2,1024]{2,1,0:T(2,128)(2,1)}), bf16[64,2,1024]{2,1,0:T(2,128)(2,1)S(1)}, u32[]{:S(2)}, u32[]{:S(2)}) async-start(bf16[64,2,1024]{2,1,0:T(2,128)(2,1)} %copy.20), calls=%async_computation | async-start | bytes 524288 | tf_op jit(solution)/shard_map/all_to_all | solution.py:131
  51.4 253.8 %all-to-all-start.2 = ((bf16[64,64,1024]{2,1,0:T(8,128)(2,1)}), bf16[64,64,1024]{2,1,0:T(8,128)(2,1)}, u32[]{:S(2)}, u32[]{:S(2)}) async-start(bf16[64,64,1024]{2,1,0:T(8,128)(2,1)} %gather_fusion.2), calls=%async_computation.2 | async-start | bytes 16777216 | tf_op jit(solution)/shard_map/all_to_all | solution.py:135
  56.8 22.8 %collective-permute-start = (bf16[64,1024]{1,0:T(8,128)(2,1)S(1)}, bf16[64,1024]{1,0:T(8,128)(2,1)S(1)}, u32[]{:S(2)}, u32[]{:S(2)}) collective-permute-start(bf16[64,1024]{1,0:T(8,128)(2,1)S(1)} %get-tuple-element.13), channel_id=1, source_target_pairs={{0,4},{4,8},{8,12},{12,16},{16,20},{20,24},{24,28},{28,32},{32,36}... | collective-permute-start | bytes 393224 | tf_op jit(solution)/shard_map/ppermute | solution.py:138
  60.4 28.5 %collective-permute-start.1 = (bf16[64,1024]{1,0:T(8,128)(2,1)S(1)}, bf16[64,1024]{1,0:T(8,128)(2,1)S(1)}, u32[]{:S(2)}, u32[]{:S(2)}) collective-permute-start(bf16[64,1024]{1,0:T(8,128)(2,1)S(1)} %get-tuple-element.14), channel_id=1, source_target_pairs={{4,0},{8,4},{12,8},{16,12},{20,16},{24,20},{28,24},{32,28},{36,32}... | collective-permute-start | bytes 393224 | tf_op jit(solution)/shard_map/ppermute | solution.py:139
  89.1 200.9 %copy-start.6 = (bf16[1024,512]{1,0:T(8,128)(2,1)S(1)}, bf16[1024,512]{1,0:T(8,128)(2,1)}, u32[]{:S(2)}) copy-start(bf16[1024,512]{1,0:T(8,128)(2,1)} %q_ref.3) | copy-start | bytes 3145732
  290.0 1.3 copy-start.4
  291.3 1.3 copy-start.5
  302.5 1.3 copy-start
  303.9 1.3 copy-start.2
  305.2 1.6 copy-start.1
  306.8 1.6 copy-start.3
  308.3 1.2 copy-start.7
Sparse Core Ops, SparseCore 0:
  9.2 160.4 all-gather.2

commit v2 on v1

v2 whole, which is shorter than its diff:
```python
import jax
import jax.numpy as jnp
from jax import lax
from jax.experimental import pallas as pl
from jax.experimental.pallas import tpu as pltpu
from jax.sharding import PartitionSpec as P

HD = 128
BLOCK = 64
G = 2
R = 3
LOW = -1e30
NT = (((1,), (1,)), ((), ()))
MESH = pl.DeviceIdType.MESH
PLANE = 8
LAYERS = 8
SHIFTS = (0, 1, -1, 2, -2, 3, -3, 4)


def lanes_of(parts):
    rows = parts[0].shape[0]
    lane = lax.broadcasted_iota(jnp.int32, (rows, HD), 1)
    out = jnp.zeros((rows, HD), jnp.float32)
    for i, part in enumerate(parts):
        out = jnp.where(lane == i, part, out)
    return out


def kernel(
    table, inverse, owners, flags, keep,
    q_ref, k_ref, v_ref,
    heads_ref,
    fetched, front1, back1, front2, back2, stage, pick3, got3, got4,
    halo, key_pad, value_pad, g_mine, g_in, g_part, g_col, g_sum, g_all,
    near_acc, near_max, near_sum, far_acc, far_max, far_sum, context,
    hop1_s, hop1_r, hop2_s, hop2_r, hop3_s, hop3_r, hop4_s, hop4_r,
    in_s, in_r, halo_s, halo_r, g_s, g_r, c_s, c_r,
):
    me = lax.axis_index("seq")
    row = lax.axis_index("fsdp")
    z, p_me = me // PLANE, me % PLANE
    count = PLANE * LAYERS
    tokens, width = key_pad.shape[0] - 2 * BLOCK, q_ref.shape[2]
    heads = width // HD
    pair = 2 * BLOCK

    def col(shift):
        return lax.rem(z + shift + LAYERS, LAYERS) * PLANE + p_me

    def mate(r):
        return lax.rem(p_me + r, PLANE)

    def from_mate(r):
        return lax.rem(p_me - r + PLANE, PLANE)

    def layer(d):
        return lax.rem(z - SHIFTS[d] + LAYERS, LAYERS)

    def copy(src, dst, send, recv, device):
        return pltpu.make_async_remote_copy(
            src_ref=src, dst_ref=dst, send_sem=send, recv_sem=recv,
            device_id={"seq": device}, device_id_type=MESH,
        )

    def cross(src, dst, send, recv, device):
        return pltpu.make_async_remote_copy(
            src_ref=src, dst_ref=dst, send_sem=send, recv_sem=recv,
            device_id={"fsdp": device}, device_id_type=MESH,
        )

    next_one, last_one = lax.rem(me + 1, count), lax.rem(me + count - 1, count)
    barrier = pltpu.get_barrier_semaphore()
    for r in range(1, PLANE):
        pl.semaphore_signal(barrier, inc=1, device_id={"seq": z * PLANE + mate(r)}, device_id_type=MESH)
    for s in range(1, LAYERS):
        pl.semaphore_signal(barrier, inc=1, device_id={"seq": col(s)}, device_id_type=MESH)
    pl.semaphore_signal(barrier, inc=1, device_id={"seq": next_one}, device_id_type=MESH)
    pl.semaphore_signal(barrier, inc=1, device_id={"seq": last_one}, device_id_type=MESH)
    for f in range(1, 4):
        pl.semaphore_signal(barrier, inc=1, device_id={"fsdp": lax.rem(row + f, 4)}, device_id_type=MESH)
    pl.semaphore_wait(barrier, 7 + 7 + 2 + 3)

    ways = (1, -1)
    first_hop, second_hop = (front1, back1), (front2, back2)
    own = (k_ref, v_ref)

    def hop1(w, t):
        return copy(own[t], first_hop[w].at[t], hop1_s.at[w, t], hop1_r.at[w, t], col(ways[w]))

    def hop2(w, t):
        return copy(first_hop[w].at[t], second_hop[w].at[t], hop2_s.at[w, t], hop2_r.at[w, t], col(ways[w]))

    def hop3(w, c):
        part = pl.ds(0, 4) if c == 0 else pl.ds(2 * c + 2, 2)
        return copy(pick3.at[w, part], got3.at[w, part], hop3_s.at[w, c], hop3_r.at[w, c], col(ways[w]))

    def hop4(w):
        return copy(got3.at[w, pl.ds(0, 4)], got4.at[w], hop4_s.at[w], hop4_r.at[w], col(ways[w]))

    for t in range(2):
        for w in range(2):
            hop1(w, t).start()

    def halo_copy(side, t):
        block = tokens // BLOCK - 1 if side == 0 else 0
        return copy(
            own[t].at[block], halo.at[side, pl.ds(t * BLOCK, BLOCK)], halo_s.at[side, t], halo_r.at[side, t],
            next_one if side == 0 else last_one,
        )

    for side in range(2):
        for t in range(2):
            halo_copy(side, t).start()

    piece = G * pair // PLANE
    for g in range(G):
        for t in range(2):
            block = own[t][flags[g]].astype(jnp.float32) * keep[g]
            g_mine[pl.ds(g * pair + t * BLOCK, BLOCK), :] = block.astype(jnp.bfloat16)

    def piece_at(p):
        return pl.ds(pl.multiple_of(p * piece, piece), piece)

    def g1(r, p):
        return copy(g_mine.at[piece_at(p)], g_in.at[r], g_s.at[0, r], g_r.at[0, r], z * PLANE + p)

    def g2(s):
        return copy(g_part, g_col.at[s], g_s.at[1, s], g_r.at[1, s], col(s))

    def g3(r, p, at):
        return copy(g_sum, g_all.at[piece_at(at)], g_s.at[2, r], g_r.at[2, r], z * PLANE + p)

    def each(low, high, body):
        def step(i, carry):
            body(i)
            return carry

        lax.fori_loop(low, high, step, 0)

    each(1, PLANE, lambda r: g1(r, mate(r)).start())
    g_in[0] = g_mine[piece_at(p_me), :]

    def choose(d, source):
        owner = layer(d) * PLANE + p_me

        def one(r):
            spot = table[z * PLANE + mate(r), owner]
            for t in range(2):
                stage[d, r, pl.ds(t * BLOCK, BLOCK), :] = source(t, spot)

        each(0, PLANE, one)
        fetched[owner] = stage[d, 0]

    def spread_one(d, r, src):
        owner = layer(d) * PLANE + p_me
        return copy(src, fetched.at[owner], in_s.at[d, r], in_r.at[d, r], z * PLANE + mate(r))

    def spread(d):
        each(1, PLANE, lambda r: spread_one(d, r, stage.at[d, r]).start())

    def arrived(d, r):
        owner = layer(d) * PLANE + from_mate(r)
        copy(fetched.at[owner], fetched.at[owner], in_s.at[d, r], in_r.at[d, r], z * PLANE + mate(r)).wait_recv()

    def columns(h):
        return pl.ds(h * HD, HD)

    def attend(owner):
        asker = inverse[owner]
        scores = []
        for h in range(heads):
            keys = fetched[owner, pl.ds(0, BLOCK), columns(h)]
            scores.append(lax.dot_general(q_ref[asker, :, columns(h)], keys, NT, preferred_element_type=jnp.float32))
        scores = jnp.concatenate(scores, axis=0) * HD**-0.5
        row_max = jnp.max(scores, axis=1, keepdims=True)
        lifted = jnp.exp(scores - row_max)
        row_sum = jnp.sum(lifted, axis=1, keepdims=True)
        lifted = lifted.astype(jnp.bfloat16)
        parts = [slice(h * BLOCK, (h + 1) * BLOCK) for h in range(heads)]
        for h in range(heads):
            values = fetched[owner, pl.ds(BLOCK, BLOCK), columns(h)]
            far_acc[owner, :, columns(h)] = jnp.dot(lifted[parts[h]], values, preferred_element_type=jnp.float32)
        far_max[owner] = lanes_of([row_max[part] for part in parts])
        far_sum[owner] = lanes_of([row_sum[part] for part in parts])

    def attend_layer(d):
        def one(r):
            @pl.when(r > 0)
            def _():
                arrived(d, r)

            attend(layer(d) * PLANE + from_mate(r))

        each(0, PLANE, one)

    choose(0, lambda t, spot: own[t][spot])
    spread(0)

    each(1, PLANE, lambda r: g1(r, mate(r)).wait_recv())
    total = g_in[0]
    for r in range(1, PLANE):
        total = total + g_in[r]
    g_part[...] = total
    each(1, LAYERS, lambda s: g2(s).start())
    g_col[0] = total

    attend_layer(0)

    for t in range(2):
        for w in range(2):
            hop1(w, t).wait_recv()
            hop2(w, t).start()
    for w in range(2):
        choose(1 + w, lambda t, spot: first_hop[w][t, spot])
        spread(1 + w)

    each(1, LAYERS, lambda s: g2(s).wait_recv())
    total = g_col[0]
    for s in range(1, LAYERS):
        total = total + g_col[s]
    g_sum[...] = total
    each(1, PLANE, lambda r: g3(r, mate(r), p_me).start())
    g_all[piece_at(p_me), :] = total

    for side in range(2):
        for t in range(2):
            halo_copy(side, t).wait_recv()
    pads = (key_pad, value_pad)
    for t in range(2):
        pads[t][pl.ds(0, BLOCK), :] = halo[0, pl.ds(t * BLOCK, BLOCK), :]
        pads[t][pl.ds(BLOCK, tokens), :] = own[t][...].reshape(tokens, width)
        pads[t][pl.ds(BLOCK + tokens, BLOCK), :] = halo[1, pl.ds(t * BLOCK, BLOCK), :]
    each(1, PLANE, lambda r: g3(r, mate(r), from_mate(r)).wait_recv())

    tile = 2 * BLOCK
    span = tile + 2 * BLOCK
    steps = tokens // tile

    def near(step):
        wide = span + G * BLOCK
        row_block = lax.broadcasted_iota(jnp.int32, (tile, wide), 0) // BLOCK
        column = lax.broadcasted_iota(jnp.int32, (tile, wide), 1)
        key_block = column // BLOCK
        first = jnp.where((me == 0) & (step == 0), 1, 0)
        last = jnp.where((me == count - 1) & (step == steps - 1), 1, 0)
        listed = (key_block >= row_block) & (key_block <= row_block + 2)
        listed = listed & (key_block >= first) & (key_block < span // BLOCK - last)
        listed = listed | (column >= span)
        rows = pl.ds(pl.multiple_of(step * tile, tile), tile)
        around = pl.ds(pl.multiple_of(step * tile, tile), span)
        maxima, sums = [], []
        for h in range(heads):
            shared = [g_all[pl.ds(b * BLOCK, BLOCK), columns(h)] for b in range(2 * G)]
            keys = jnp.concatenate([key_pad[around, columns(h)]] + shared[0::2], axis=0)
            values = jnp.concatenate([value_pad[around, columns(h)]] + shared[1::2], axis=0)
            query = q_ref[pl.ds(step * (tile // BLOCK), tile // BLOCK), :, columns(h)].reshape(tile, HD)
            scores = lax.dot_general(query, keys, NT, preferred_element_type=jnp.float32)
            scores = jnp.where(listed, scores * HD**-0.5, LOW)
            row_max = jnp.max(scores, axis=1, keepdims=True)
            lifted = jnp.exp(scores - row_max)
            maxima.append(row_max)
            sums.append(jnp.sum(lifted, axis=1, keepdims=True))
            near_acc[rows, columns(h)] = jnp.dot(
                lifted.astype(jnp.bfloat16), values, preferred_element_type=jnp.float32
            )
        near_max[rows, :] = lanes_of(maxima)
        near_sum[rows, :] = lanes_of(sums)

    each(0, steps, near)
    for w in range(2):
        attend_layer(1 + w)

    for w in range(2):
        for t in range(2):
            hop2(w, t).wait_recv()
        way = ways[w]
        owner = col(-2 * way)

        def one(j, r, far):
            to = lax.rem(z + far * way + LAYERS, LAYERS) * PLANE + mate(r)
            spot = table[to, owner]
            for t in range(2):
                pick3[w, j, pl.ds(t * BLOCK, BLOCK), :] = second_hop[w][t, spot]

        each(0, 4, lambda j: one(j, 2 * j + w, 2))
        each(0, PLANE, lambda r: one(4 + r, r, 1))
        for c in range(5):
            hop3(w, c).start()
    for w in range(2):
        choose(3 + w, lambda t, spot: second_hop[w][t, spot])
        spread(3 + w)
    for w in range(2):
        hop3(w, 0).wait_recv()
        hop4(w).start()
    for c in range(1, 5):
        for w in range(2):
            hop3(w, c).wait_recv()
            for r in (2 * c - 2, 2 * c - 1):
                if r == 0:
                    fetched[layer(5 + w) * PLANE + p_me] = got3[w, 4]
                else:
                    spread_one(5 + w, r, got3.at[w, 4 + r]).start()
        if c <= 2:
            attend_layer(2 + c)
    for w in range(2):
        hop4(w).wait_recv()
    for r in range(PLANE):
        if r == 0:
            fetched[layer(7) * PLANE + p_me] = got4[0, 0]
        else:
            spread_one(7, r, got4.at[r % 2, r // 2]).start()
    attend_layer(5)
    attend_layer(6)
    attend_layer(7)

    quarter = tokens // 4

    def merge(block):
        rows = pl.ds(pl.multiple_of(block * BLOCK, BLOCK), BLOCK)
        slots = [owners[block * R + j] for j in range(R)]
        maxima = [near_max[rows, :]] + [far_max[slot] for slot in slots]
        top = maxima[0]
        for one in maxima[1:]:
            top = jnp.maximum(top, one)
        scales = [jnp.exp(one - top) for one in maxima]
        sums = [near_sum[rows, :]] + [far_sum[slot] for slot in slots]
        whole = scales[0] * sums[0]
        for scale, one in zip(scales[1:], sums[1:]):
            whole = whole + scale * one
        scales = [scale / whole for scale in scales]
        for h in range(heads):
            out = scales[0][:, h : h + 1] * near_acc[rows, columns(h)]
            for scale, slot in zip(scales[1:], slots):
                out = out + scale[:, h : h + 1] * far_acc[slot, :, columns(h)]
            context[rows, columns(h)] = out.astype(jnp.bfloat16)

    def quarter_at(f):
        return pl.ds(pl.multiple_of(f * quarter, quarter), quarter)

    def heads_at(f):
        return pl.ds(pl.multiple_of(f * width, width), width)

    blocks = quarter // BLOCK
    for f in (2, 1, 3, 0):
        to = lax.rem(row + f, 4)
        each(0, blocks, lambda b: merge(to * blocks + b))
        if f > 0:
            cross(context.at[quarter_at(to)], heads_ref.at[:, heads_at(row)], c_s.at[f], c_r.at[f], to).start()
        else:
            heads_ref[:, heads_at(row)] = context[quarter_at(row), :]

    for t in range(2):
        for w in range(2):
            hop1(w, t).wait_send()
            hop2(w, t).wait_send()
    for w in range(2):
        for c in range(5):
            hop3(w, c).wait_send()
        hop4(w).wait_send()
    for side in range(2):
        for t in range(2):
            halo_copy(side, t).wait_send()
    for d in range(LAYERS):
        each(1, PLANE, lambda r: spread_one(d, r, fetched.at[0]).wait_send())
    each(1, PLANE, lambda r: g1(r, mate(r)).wait_send())
    each(1, LAYERS, lambda s: g2(s).wait_send())
    each(1, PLANE, lambda r: g3(r, mate(r), p_me).wait_send())
    for f in range(1, 4):
        cross(context.at[quarter_at(0)], heads_ref.at[:, heads_at(row)], c_s.at[f], c_r.at[f], row).wait_send()
        came = lax.rem(row - f + 4, 4)
        cross(context.at[quarter_at(0)], heads_ref.at[:, heads_at(came)], c_s.at[f], c_r.at[f], row).wait_recv()


def gather_attend(table, inverse, owners, flags, keep, query, keys, values):
    tokens, width = query.shape[0] * BLOCK, query.shape[2]
    n = table.shape[0]
    pair = 2 * BLOCK
    piece = G * pair // PLANE
    half, full = jnp.bfloat16, jnp.float32
    vmem = pl.BlockSpec(memory_space=pltpu.VMEM)
    smem = pl.BlockSpec(memory_space=pltpu.SMEM)
    sem = pltpu.SemaphoreType.DMA
    hop = pltpu.VMEM((2,) + query.shape, half)
    return pl.pallas_call(
        kernel,
        out_shape=jax.ShapeDtypeStruct((tokens // 4, 4 * width), half),
        in_specs=[smem] * 5 + [vmem] * 3,
        out_specs=vmem,
        scratch_shapes=[
            pltpu.VMEM((n, pair, width), half),
            hop, hop, hop, hop,
            pltpu.VMEM((5, PLANE, pair, width), half),
            pltpu.VMEM((2, 12, pair, width), half),
            pltpu.VMEM((2, 12, pair, width), half),
            pltpu.VMEM((2, 4, pair, width), half),
            pltpu.VMEM((2, pair, width), half),
            pltpu.VMEM((tokens + pair, width), half),
            pltpu.VMEM((tokens + pair, width), half),
            pltpu.VMEM((G * pair, width), half),
            pltpu.VMEM((PLANE, piece, width), half),
            pltpu.VMEM((piece, width), half),
            pltpu.VMEM((LAYERS, piece, width), half),
            pltpu.VMEM((piece, width), half),
            pltpu.VMEM((G * pair, width), half),
            pltpu.VMEM((tokens, width), full),
            pltpu.VMEM((tokens, HD), full),
            pltpu.VMEM((tokens, HD), full),
            pltpu.VMEM((n, BLOCK, width), full),
            pltpu.VMEM((n, BLOCK, HD), full),
            pltpu.VMEM((n, BLOCK, HD), full),
            pltpu.VMEM((tokens, width), half),
            sem((2, 2)), sem((2, 2)), sem((2, 2)), sem((2, 2)),
            sem((2, 5)), sem((2, 5)), sem((2,)), sem((2,)),
            sem((LAYERS, PLANE)), sem((LAYERS, PLANE)),
            sem((2, 2)), sem((2, 2)), sem((3, 8)), sem((3, 8)), sem((4,)), sem((4,)),
        ],
        compiler_params=pltpu.CompilerParams(
            collective_id=0, has_side_effects=True, vmem_limit_bytes=58 << 20
        ),
        cost_estimate=pl.CostEstimate(flops=3 * 10**9, bytes_accessed=10 * 10**6, transcendentals=4 * 10**6),
    )(table, inverse, owners, flags, keep, query, keys, values)


def on_device(query_rows, key_rows, value_rows, out_weight, random_ids, global_ids):
    tokens, width = query_rows.shape
    n = lax.axis_size("seq")
    blocks = tokens // BLOCK
    me = lax.axis_index("seq")
    flat = random_ids.reshape(-1)
    owners, spots = flat // blocks, flat % blocks
    hits = owners[:, None] == jnp.arange(n)[None, :]
    mine = jnp.sum(jnp.where(hits, spots[:, None], 0), axis=0)
    inverse = jnp.sum(jnp.where(hits, (jnp.arange(flat.shape[0]) // R)[:, None], 0), axis=0)
    table = lax.all_to_all(
        jnp.broadcast_to(mine[None], (n, n)), "seq", split_axis=0, concat_axis=0, tiled=True
    )
    flags = global_ids % blocks
    keep = (global_ids // blocks == me).astype(jnp.float32)
    weight = lax.all_gather(out_weight, "fsdp", axis=0, tiled=True)
    rows = [array.reshape(blocks, BLOCK, width) for array in (query_rows, key_rows, value_rows)]
    all_heads = gather_attend(table, inverse, owners, flags, keep, *rows)
    return jnp.dot(all_heads, weight, preferred_element_type=jnp.float32).astype(jnp.bfloat16)


def solution(mesh):
    return jax.shard_map(
        on_device,
        mesh=mesh,
        in_specs=(
            P("seq", "fsdp"),
            P("seq", "fsdp"),
            P("seq", "fsdp"),
            P("fsdp", None),
            P("seq", None),
            P(),
        ),
        out_specs=P(("seq", "fsdp"), None),
        check_vma=False,
    )
```

time: 375 us -> 236 us (0.63)
  blocking collectives: 217 us -> 0 us
  Pallas kernels: 36.8 us -> 184 us
  waiting for transfers between devices: 43 us -> 7.59 us
  local copies, waits for them, and re-layouts: 21.6 us -> 2.09 us
  starting transfers between devices: 28.6 us -> 13 us
    all_gather x1 -> x0, blocking collectives: 198 us -> none  [on_device(): lax.all_gather(piece, 'seq', axis=1, tiled=False)]
    pallas_call x2 -> x1, Pallas kernels: 36.8 us -> 184 us  [gather_attend(): pl.pallas_call(kernel, out_shape=jax.ShapeDtypeStruct((tokens // 4, 4 * w...]
    ppermute x2 -> x0, waiting for transfers between devices: 26.5 us -> none  [the longest x1 17.3 us: on_device(): before = lax.ppermute(pair[-BLOCK:], 'seq', up)]
    all_to_all x1 -> x0, blocking collectives: 18.7 us -> none  [on_device(): lax.all_to_all(context, 'fsdp', split_axis=0, concat_axis=1, tiled=True)]
    all_to_all x3 -> x1, starting transfers between devices: 23.2 us -> 13 us  [on_device(): lax.all_to_all(jnp.broadcast_to(mine[None], (n, n)), 'seq', split_axis=0,...]
    unnamed x26 -> x5, local copies, waits for them, and re-layouts: 10.8 us -> 1.37 us
    all_to_all x3 -> x1, waiting for transfers between devices: 15.9 us -> 6.86 us  [on_device(): lax.all_to_all(jnp.broadcast_to(mine[None], (n, n)), 'seq', split_axis=0,...]
    gather x3 -> x0, local copies, waits for them, and re-layouts: 6.48 us -> none  [the longest x1 5.31 us: on_device(): served = pair_blocks[wanted]]
  transfers between devices with their start and end apart: 6 -> 2, of which waited for: 4 -> 1; matrix products, arithmetic and copies ran while one was open for 3% -> 2% of each run, Pallas kernels for 10% -> 78%
where the time goes in v2:
time: 236 us; the launch traced here: 235 us
  Pallas kernels  184 us (78%)
  between operations  13.4 us (6%)
  starting transfers between devices  13 us (6%)
  matrix products  11.9 us (5%)
  waiting for transfers between devices  7.59 us (3%)
  other arithmetic  3.13 us (1%)
    pallas_call x1, Pallas kernels, gather_attend(): pl.pallas_call(kernel, out_shape=jax.ShapeDtypeStruct((tokens // 4, 4 * w...  184 us
    all_to_all x1, starting transfers between devices, on_device(): lax.all_to_all(jnp.broadcast_to(mine[None], (n, n)), 'seq', split_axis=0,...  13 us
    dot_general x1, matrix products, on_device(): jnp.dot(all_heads, weight, preferred_element_type=jnp.float32)  11.9 us
    all_to_all x1, waiting for transfers between devices, on_device(): lax.all_to_all(jnp.broadcast_to(mine[None], (n, n)), 'seq', split_axis=0,...  6.86 us
  transfers between devices with their start and end apart: 2, of which 1 were waited for; matrix products, arithmetic and copies ran while one was open for 2% of the time, Pallas kernels for 78%

profile of v2, /device:TPU:1, one launch (start us, length us, event | category | flops | bytes accessed | tf_op | source)
XLA Modules:
  0.0 235.4 jit_solution(15906617192292262284)
XLA Ops:
  6.5 0.0 all-gather.2.cloned.1.call-start
  6.5 0.7 all-gather.2.cloned.1.call-update
  7.3 0.8 copy.10
  8.0 0.1 reshape.80
  8.1 0.0 copy-start.1
  8.1 0.7 select_reduce_fusion
  8.8 0.6 broadcast_in_dim.30
  9.4 13.0 %all-to-all-start = ((s32[64,1,64]{2,1,0:T(1,128)}), s32[64,1,64]{2,1,0:T(1,128)S(1)}, u32[]{:S(2)}, u32[]{:S(2)}) async-start(s32[64,1,64]{2,1,0:T(1,128)} %broadcast_in_dim.30), calls=%async_computation | async-start | bytes 65536 | tf_op jit(solution)/shard_map/all_to_all | solution.py:434
  22.4 1.2 and_select_fusion.1.flags
  23.6 1.2 compare_convert_fusion.keep
  24.9 6.9 %all-to-all-done = s32[64,1,64]{2,1,0:T(1,128)S(1)} async-done(((s32[64,1,64]{2,1,0:T(1,128)}), s32[64,1,64]{2,1,0:T(1,128)S(1)}, u32[]{:S(2)}, u32[]{:S(2)}) %all-to-all-start) | async-done | bytes 16416 | tf_op jit(solution)/shard_map/all_to_all | solution.py:434
  31.7 0.0 copy-start
  31.7 0.0 copy-done.1
  31.7 0.6 copy-done
  32.4 184.3 %shard_map.64 = bf16[256,2048]{1,0:T(8,128)(2,1)} custom-call(s32[64,64]{1,0:T(8,128)} %bitcast.6, s32[64]{0:T(128)} %get-tuple-element.5.inverse, s32[48]{0:T(128)} %copy-done.1, s32[2]{0:T(128)} %and_select_fusion.1.flags, f32[2]{0:T(128)} %compare_convert_fusion.keep, bf16[16,64,512]{2,1,0:T(8,128)(2,1)} %bitcast.7, bf16[16,64,512]{2,1,0:T(8,128)(2,1)} %bitcast.8, ...), custom_call_target="tpu_custom_call" | custom-call | flops 3000000000 | bytes 10000000 | tf_op jit(solution)/shard_map/pallas_call | solution.py:384
  216.6 0.0 all-gather.2.cloned.1.call-done
  216.7 11.9 %convolution_convert_fusion = bf16[256,4096]{1,0:T(8,128)(2,1)} fusion(bf16[256,2048]{1,0:T(8,128)(2,1)} %shard_map.64, bf16[2048,4096]{1,0:T(8,128)(2,1)} %all-gather.2.cloned.1.call-done), kind=kOutput, calls=%fused_computation | convolution fusion | flops 4296015872 | bytes 19922944 | tf_op jit(solution)/shard_map/dot_general | solution.py:442
  (1 shorter events, 0.0 us)
Async XLA Ops:
  6.5 210.1 %all-gather.2.cloned.1.call-start = ((), (), s32[]{:S(2)}) async-start(), calls=%async_computation.1 | async-start | bytes 20971520 | tf_op jit(solution)/shard_map/all_gather | solution.py:439
  8.1 23.6 %copy-start.1 = (s32[48]{0:T(128)}, s32[48]{0:T(128)S(1)}, u32[]{:S(2)}) copy-start(s32[48]{0:T(128)S(1)} %get-tuple-element.8.owners) | copy-start | bytes 580
  9.4 22.3 %all-to-all-start = ((s32[64,1,64]{2,1,0:T(1,128)}), s32[64,1,64]{2,1,0:T(1,128)S(1)}, u32[]{:S(2)}, u32[]{:S(2)}) async-start(s32[64,1,64]{2,1,0:T(1,128)} %broadcast_in_dim.30), calls=%async_computation | async-start | bytes 65536 | tf_op jit(solution)/shard_map/all_to_all | solution.py:434
  31.7 0.6 copy-start
Sparse Core Ops, SparseCore 0:
  9.2 160.4 all-gather.1

commit v3 on v2

--- a/solution.py
+++ b/solution.py
@@ -27,14 +27,15 @@
 
 
 def kernel(
-    table, inverse, owners, flags, keep,
+    ids, shared_ids,
     q_ref, k_ref, v_ref,
     heads_ref,
     fetched, front1, back1, front2, back2, stage, pick3, got3, got4,
     halo, key_pad, value_pad, g_mine, g_in, g_part, g_col, g_sum, g_all,
     near_acc, near_max, near_sum, far_acc, far_max, far_sum, context,
+    mine_v, inverse_v, table_v, tables_v, inverse, table, tables,
     hop1_s, hop1_r, hop2_s, hop2_r, hop3_s, hop3_r, hop4_s, hop4_r,
-    in_s, in_r, halo_s, halo_r, g_s, g_r, c_s, c_r,
+    in_s, in_r, halo_s, halo_r, g_s, g_r, c_s, c_r, t_s, t_r, far_s, far_r, local_s,
 ):
     me = lax.axis_index("seq")
     row = lax.axis_index("fsdp")
@@ -112,10 +113,39 @@
         for t in range(2):
             halo_copy(side, t).start()
 
+    blocks_here = ids.shape[0]
+    lane = lax.broadcasted_iota(jnp.int32, mine_v.shape, 1)
+    wanted = jnp.zeros(mine_v.shape, jnp.int32)
+    askers = jnp.zeros(mine_v.shape, jnp.int32)
+    for b in range(blocks_here):
+        for j in range(R):
+            hit = lane == lax.div(ids[b, j], blocks_here)
+            wanted = jnp.where(hit, lax.rem(ids[b, j], blocks_here), wanted)
+            askers = jnp.where(hit, b, askers)
+    mine_v[...] = wanted
+    inverse_v[...] = askers
+
+    def row_copy(r, at):
+        return copy(mine_v, table_v.at[at], t_s.at[r], t_r.at[r], z * PLANE + mate(r))
+
+    def table_copy(w, far):
+        k = 2 * w + far - 1
+        return copy(table_v, tables_v.at[k], far_s.at[k], far_r.at[k], col(-far * ways[w]))
+
+    for r in range(1, PLANE):
+        row_copy(r, p_me).start()
+    table_v[p_me] = wanted
+    keep_inverse = pltpu.make_async_copy(inverse_v, inverse, local_s.at[0])
+    keep_table = pltpu.make_async_copy(table_v, table, local_s.at[1])
+    keep_tables = pltpu.make_async_copy(tables_v, tables, local_s.at[2])
+    keep_inverse.start()
+
     piece = G * pair // PLANE
     for g in range(G):
+        holder = jnp.full((BLOCK, width), lax.div(shared_ids[g], blocks_here), jnp.int32)
+        keep = jnp.where(holder == me, 1.0, 0.0)
         for t in range(2):
-            block = own[t][flags[g]].astype(jnp.float32) * keep[g]
+            block = own[t][lax.rem(shared_ids[g], blocks_here)].astype(jnp.float32) * keep
             g_mine[pl.ds(g * pair + t * BLOCK, BLOCK), :] = block.astype(jnp.bfloat16)
 
     def piece_at(p):
@@ -144,7 +174,7 @@
         owner = layer(d) * PLANE + p_me
 
         def one(r):
-            spot = table[z * PLANE + mate(r), owner]
+            spot = table[mate(r), 0, owner]
             for t in range(2):
                 stage[d, r, pl.ds(t * BLOCK, BLOCK), :] = source(t, spot)
 
@@ -166,7 +196,7 @@
         return pl.ds(h * HD, HD)
 
     def attend(owner):
-        asker = inverse[owner]
+        asker = inverse[0, owner]
         scores = []
         for h in range(heads):
             keys = fetched[owner, pl.ds(0, BLOCK), columns(h)]
@@ -193,6 +223,14 @@
 
         each(0, PLANE, one)
 
+    for r in range(1, PLANE):
+        row_copy(r, from_mate(r)).wait_recv()
+    keep_table.start()
+    for w in range(2):
+        for far in (1, 2):
+            table_copy(w, far).start()
+    keep_inverse.wait()
+    keep_table.wait()
     choose(0, lambda t, spot: own[t][spot])
     spread(0)
 
@@ -271,14 +309,17 @@
         attend_layer(1 + w)
 
     for w in range(2):
+        for far in (1, 2):
+            table_copy(w, far).wait_recv()
+    keep_tables.start()
+    keep_tables.wait()
+    for w in range(2):
         for t in range(2):
             hop2(w, t).wait_recv()
-        way = ways[w]
-        owner = col(-2 * way)
+        owner = col(-2 * ways[w])
 
         def one(j, r, far):
-            to = lax.rem(z + far * way + LAYERS, LAYERS) * PLANE + mate(r)
-            spot = table[to, owner]
+            spot = tables[2 * w + far - 1, mate(r), 0, owner]
             for t in range(2):
                 pick3[w, j, pl.ds(t * BLOCK, BLOCK), :] = second_hop[w][t, spot]
 
@@ -317,7 +358,7 @@
 
     def merge(block):
         rows = pl.ds(pl.multiple_of(block * BLOCK, BLOCK), BLOCK)
-        slots = [owners[block * R + j] for j in range(R)]
+        slots = [lax.div(ids[block, j], blocks_here) for j in range(R)]
         maxima = [near_max[rows, :]] + [far_max[slot] for slot in slots]
         top = maxima[0]
         for one in maxima[1:]:
@@ -365,15 +406,20 @@
     each(1, PLANE, lambda r: g1(r, mate(r)).wait_send())
     each(1, LAYERS, lambda s: g2(s).wait_send())
     each(1, PLANE, lambda r: g3(r, mate(r), p_me).wait_send())
+    for r in range(1, PLANE):
+        row_copy(r, p_me).wait_send()
+    for w in range(2):
+        for far in (1, 2):
+            table_copy(w, far).wait_send()
     for f in range(1, 4):
         cross(context.at[quarter_at(0)], heads_ref.at[:, heads_at(row)], c_s.at[f], c_r.at[f], row).wait_send()
         came = lax.rem(row - f + 4, 4)
         cross(context.at[quarter_at(0)], heads_ref.at[:, heads_at(came)], c_s.at[f], c_r.at[f], row).wait_recv()
 
 
-def gather_attend(table, inverse, owners, flags, keep, query, keys, values):
+def gather_attend(ids, shared_ids, query, keys, values):
     tokens, width = query.shape[0] * BLOCK, query.shape[2]
-    n = table.shape[0]
+    n = PLANE * LAYERS
     pair = 2 * BLOCK
     piece = G * pair // PLANE
     half, full = jnp.bfloat16, jnp.float32
@@ -384,7 +430,7 @@
     return pl.pallas_call(
         kernel,
         out_shape=jax.ShapeDtypeStruct((tokens // 4, 4 * width), half),
-        in_specs=[smem] * 5 + [vmem] * 3,
+        in_specs=[smem] * 2 + [vmem] * 3,
         out_specs=vmem,
         scratch_shapes=[
             pltpu.VMEM((n, pair, width), half),
@@ -409,36 +455,32 @@
             pltpu.VMEM((n, BLOCK, HD), full),
             pltpu.VMEM((n, BLOCK, HD), full),
             pltpu.VMEM((tokens, width), half),
+            pltpu.VMEM((PLANE, HD), jnp.int32),
+            pltpu.VMEM((PLANE, HD), jnp.int32),
+            pltpu.VMEM((PLANE, PLANE, HD), jnp.int32),
+            pltpu.VMEM((4, PLANE, PLANE, HD), jnp.int32),
+            pltpu.SMEM((PLANE, HD), jnp.int32),
+            pltpu.SMEM((PLANE, PLANE, HD), jnp.int32),
+            pltpu.SMEM((4, PLANE, PLANE, HD), jnp.int32),
             sem((2, 2)), sem((2, 2)), sem((2, 2)), sem((2, 2)),
             sem((2, 5)), sem((2, 5)), sem((2,)), sem((2,)),
             sem((LAYERS, PLANE)), sem((LAYERS, PLANE)),
             sem((2, 2)), sem((2, 2)), sem((3, 8)), sem((3, 8)), sem((4,)), sem((4,)),
+            sem((PLANE,)), sem((PLANE,)), sem((4,)), sem((4,)), sem((3,)),
         ],
         compiler_params=pltpu.CompilerParams(
             collective_id=0, has_side_effects=True, vmem_limit_bytes=58 << 20
         ),
         cost_estimate=pl.CostEstimate(flops=3 * 10**9, bytes_accessed=10 * 10**6, transcendentals=4 * 10**6),
-    )(table, inverse, owners, flags, keep, query, keys, values)
+    )(ids, shared_ids, query, keys, values)
 
 
 def on_device(query_rows, key_rows, value_rows, out_weight, random_ids, global_ids):
     tokens, width = query_rows.shape
-    n = lax.axis_size("seq")
     blocks = tokens // BLOCK
-    me = lax.axis_index("seq")
-    flat = random_ids.reshape(-1)
-    owners, spots = flat // blocks, flat % blocks
-    hits = owners[:, None] == jnp.arange(n)[None, :]
-    mine = jnp.sum(jnp.where(hits, spots[:, None], 0), axis=0)
-    inverse = jnp.sum(jnp.where(hits, (jnp.arange(flat.shape[0]) // R)[:, None], 0), axis=0)
-    table = lax.all_to_all(
-        jnp.broadcast_to(mine[None], (n, n)), "seq", split_axis=0, concat_axis=0, tiled=True
-    )
-    flags = global_ids % blocks
-    keep = (global_ids // blocks == me).astype(jnp.float32)
     weight = lax.all_gather(out_weight, "fsdp", axis=0, tiled=True)
     rows = [array.reshape(blocks, BLOCK, width) for array in (query_rows, key_rows, value_rows)]
-    all_heads = gather_attend(table, inverse, owners, flags, keep, *rows)
+    all_heads = gather_attend(random_ids, global_ids, *rows)
     return jnp.dot(all_heads, weight, preferred_element_type=jnp.float32).astype(jnp.bfloat16)
 
 

time: 236 us -> 221 us (0.936)
  starting transfers between devices: 13 us -> 0.01 us
  Pallas kernels: 184 us -> 193 us
  waiting for transfers between devices: 7.59 us -> 0.73 us
  other arithmetic: 3.13 us -> 0 us
    all_to_all x1 -> x0, starting transfers between devices: 13 us -> none  [on_device(): lax.all_to_all(jnp.broadcast_to(mine[None], (n, n)), 'seq', split_axis=0,...]
    pallas_call x1, Pallas kernels: 184 us -> 193 us  [gather_attend(): pl.pallas_call(kernel, out_shape=jax.ShapeDtypeStruct((tokens // 4, 4 * w...]
    all_to_all x1 -> x0, waiting for transfers between devices: 6.86 us -> none  [on_device(): lax.all_to_all(jnp.broadcast_to(mine[None], (n, n)), 'seq', split_axis=0,...]
  transfers between devices with their start and end apart: 2 -> 1, of which waited for: 1 -> 0; matrix products, arithmetic and copies ran while one was open for 2% -> 1% of each run, Pallas kernels for 78% -> 88%
where the time goes in v3:
time: 221 us; the launch traced here: 220 us
  Pallas kernels  193 us (87%)
  between operations  13.4 us (6%)
  matrix products  11.9 us (5%)
    pallas_call x1, Pallas kernels, gather_attend(): pl.pallas_call(kernel, out_shape=jax.ShapeDtypeStruct((tokens // 4, 4 * w...  193 us
    dot_general x1, matrix products, on_device(): jnp.dot(all_heads, weight, preferred_element_type=jnp.float32)  11.9 us
  transfers between devices with their start and end apart: 1, of which 0 were waited for; matrix products, arithmetic and copies ran while one was open for 1% of the time, Pallas kernels for 88%

profile of v3, /device:TPU:1, one launch (start us, length us, event | category | flops | bytes accessed | tf_op | source)
XLA Modules:
  0.0 220.4 jit_solution(7554631342003142364)
XLA Ops:
  6.5 0.0 all-gather.2.cloned.1.call-start
  6.5 0.7 all-gather.2.cloned.1.call-update
  7.3 1.4 copy.7.ids
  8.6 193.0 %shard_map.64 = bf16[256,2048]{1,0:T(8,128)(2,1)} custom-call(s32[16,3]{1,0:T(8,128)} %copy.7.ids, s32[2]{0:T(128)} %shared_ids.1, bf16[16,64,512]{2,1,0:T(8,128)(2,1)} %bitcast.5, bf16[16,64,512]{2,1,0:T(8,128)(2,1)} %bitcast.6, bf16[16,64,512]{2,1,0:T(8,128)(2,1)} %bitcast.7), custom_call_target="tpu_custom_call" | custom-call | flops 3000000000 | bytes 10000000 | tf_op jit(solution)/shard_map/pallas_call | solution.py:430
  201.6 0.0 all-gather.2.cloned.1.call-done
  201.6 11.9 %convolution_convert_fusion = bf16[256,4096]{1,0:T(8,128)(2,1)} fusion(bf16[256,2048]{1,0:T(8,128)(2,1)} %shard_map.64, bf16[2048,4096]{1,0:T(8,128)(2,1)} %all-gather.2.cloned.1.call-done), kind=kOutput, calls=%fused_computation | convolution fusion | flops 4296015872 | bytes 19922944 | tf_op jit(solution)/shard_map/dot_general | solution.py:484
Async XLA Ops:
  6.5 195.1 %all-gather.2.cloned.1.call-start = ((), (), s32[]{:S(2)}) async-start(), calls=%async_computation | async-start | bytes 20971520 | tf_op jit(solution)/shard_map/all_gather | solution.py:481
Sparse Core Ops, SparseCore 0:
  9.2 160.4 all-gather.1

commit v4 on v3

--- a/solution.py
+++ b/solution.py
@@ -28,14 +28,16 @@
 
 def kernel(
     ids, shared_ids,
-    q_ref, k_ref, v_ref,
-    heads_ref,
-    fetched, front1, back1, front2, back2, stage, pick3, got3, got4,
+    q_ref, k_ref, v_ref, w_ref,
+    heads_ref, weight_ref,
+    fetched,
+    front1_k, front1_v, back1_k, back1_v, front2_k, front2_v, back2_k, back2_v, stage, pick3, got3, got4,
     halo, key_pad, value_pad, g_mine, g_in, g_part, g_col, g_sum, g_all,
     near_acc, near_max, near_sum, far_acc, far_max, far_sum, context,
     mine_v, inverse_v, table_v, tables_v, inverse, table, tables,
     hop1_s, hop1_r, hop2_s, hop2_r, hop3_s, hop3_r, hop4_s, hop4_r,
     in_s, in_r, halo_s, halo_r, g_s, g_r, c_s, c_r, t_s, t_r, far_s, far_r, local_s,
+    row_s, row_r, core_s, core_r,
 ):
     me = lax.axis_index("seq")
     row = lax.axis_index("fsdp")
@@ -82,25 +84,48 @@
     pl.semaphore_wait(barrier, 7 + 7 + 2 + 3)
 
     ways = (1, -1)
-    first_hop, second_hop = (front1, back1), (front2, back2)
+    first_hop = ((front1_k, front1_v), (back1_k, back1_v))
+    second_hop = ((front2_k, front2_v), (back2_k, back2_v))
     own = (k_ref, v_ref)
 
     def hop1(w, t):
-        return copy(own[t], first_hop[w].at[t], hop1_s.at[w, t], hop1_r.at[w, t], col(ways[w]))
+        return copy(own[t], first_hop[w][t], hop1_s.at[w, t], hop1_r.at[w, t], col(ways[w]))
 
     def hop2(w, t):
-        return copy(first_hop[w].at[t], second_hop[w].at[t], hop2_s.at[w, t], hop2_r.at[w, t], col(ways[w]))
-
-    def hop3(w, c):
-        part = pl.ds(0, 4) if c == 0 else pl.ds(2 * c + 2, 2)
-        return copy(pick3.at[w, part], got3.at[w, part], hop3_s.at[w, c], hop3_r.at[w, c], col(ways[w]))
-
-    def hop4(w):
-        return copy(got3.at[w, pl.ds(0, 4)], got4.at[w], hop4_s.at[w], hop4_r.at[w], col(ways[w]))
+        return copy(first_hop[w][t], second_hop[w][t], hop2_s.at[w, t], hop2_r.at[w, t], col(ways[w]))
+
+    def hop3(w, t, c):
+        part = pl.ds(4 * c, 4)
+        return copy(
+            pick3.at[w, t, part], got3.at[w, t, part], hop3_s.at[w, t, c], hop3_r.at[w, t, c], col(ways[w])
+        )
+
+    def hop4(w, t):
+        return copy(got3.at[w, t, pl.ds(0, 4)], got4.at[w, t], hop4_s.at[w, t], hop4_r.at[w, t], col(ways[w]))
+
+    core = lax.rem(me, 2)
+    depth = w_ref.shape[0]
+    part_rows = pl.ds(pl.multiple_of(core * (depth // 2), depth // 2), depth // 2)
+
+    def row_weight(f, at):
+        return cross(
+            w_ref.at[part_rows], weight_ref.at[at, part_rows], row_s.at[f], row_r.at[f], lax.rem(row + f, 4)
+        )
+
+    def core_weight(f, rows):
+        came = lax.rem(row - f + 4, 4)
+        return copy(
+            weight_ref.at[came, rows], weight_ref.at[came, rows], core_s.at[f], core_r.at[f], me + 1 - 2 * core
+        )
+
+    own_weight = pltpu.make_async_copy(w_ref, weight_ref.at[row], local_s.at[3])
 
     for t in range(2):
         for w in range(2):
             hop1(w, t).start()
+    for f in (1, 3, 2):
+        row_weight(f, row).start()
+    own_weight.start()
 
     def halo_copy(side, t):
         block = tokens // BLOCK - 1 if side == 0 else 0
@@ -170,27 +195,27 @@
     each(1, PLANE, lambda r: g1(r, mate(r)).start())
     g_in[0] = g_mine[piece_at(p_me), :]
 
-    def choose(d, source):
+    def choose(d, t, read):
         owner = layer(d) * PLANE + p_me
 
         def one(r):
-            spot = table[mate(r), 0, owner]
-            for t in range(2):
-                stage[d, r, pl.ds(t * BLOCK, BLOCK), :] = source(t, spot)
+            stage[d, t, r] = read(table[mate(r), 0, owner])
 
         each(0, PLANE, one)
-        fetched[owner] = stage[d, 0]
-
-    def spread_one(d, r, src):
+        fetched[t, owner] = stage[d, t, 0]
+
+    def spread_one(d, t, r, src):
         owner = layer(d) * PLANE + p_me
-        return copy(src, fetched.at[owner], in_s.at[d, r], in_r.at[d, r], z * PLANE + mate(r))
-
-    def spread(d):
-        each(1, PLANE, lambda r: spread_one(d, r, stage.at[d, r]).start())
+        return copy(src, fetched.at[t, owner], in_s.at[t, d, r], in_r.at[t, d, r], z * PLANE + mate(r))
+
+    def spread(d, t):
+        each(1, PLANE, lambda r: spread_one(d, t, r, stage.at[d, t, r]).start())
 
     def arrived(d, r):
         owner = layer(d) * PLANE + from_mate(r)
-        copy(fetched.at[owner], fetched.at[owner], in_s.at[d, r], in_r.at[d, r], z * PLANE + mate(r)).wait_recv()
+        for t in range(2):
+            spot = fetched.at[t, owner]
+            copy(spot, spot, in_s.at[t, d, r], in_r.at[t, d, r], z * PLANE + mate(r)).wait_recv()
 
     def columns(h):
         return pl.ds(h * HD, HD)
@@ -199,7 +224,7 @@
         asker = inverse[0, owner]
         scores = []
         for h in range(heads):
-            keys = fetched[owner, pl.ds(0, BLOCK), columns(h)]
+            keys = fetched[0, owner, :, columns(h)]
             scores.append(lax.dot_general(q_ref[asker, :, columns(h)], keys, NT, preferred_element_type=jnp.float32))
         scores = jnp.concatenate(scores, axis=0) * HD**-0.5
         row_max = jnp.max(scores, axis=1, keepdims=True)
@@ -208,7 +233,7 @@
         lifted = lifted.astype(jnp.bfloat16)
         parts = [slice(h * BLOCK, (h + 1) * BLOCK) for h in range(heads)]
         for h in range(heads):
-            values = fetched[owner, pl.ds(BLOCK, BLOCK), columns(h)]
+            values = fetched[1, owner, :, columns(h)]
             far_acc[owner, :, columns(h)] = jnp.dot(lifted[parts[h]], values, preferred_element_type=jnp.float32)
         far_max[owner] = lanes_of([row_max[part] for part in parts])
         far_sum[owner] = lanes_of([row_sum[part] for part in parts])
@@ -231,8 +256,9 @@
             table_copy(w, far).start()
     keep_inverse.wait()
     keep_table.wait()
-    choose(0, lambda t, spot: own[t][spot])
-    spread(0)
+    for t in range(2):
+        choose(0, t, lambda spot: own[t][spot])
+        spread(0, t)
 
     each(1, PLANE, lambda r: g1(r, mate(r)).wait_recv())
     total = g_in[0]
@@ -248,9 +274,9 @@
         for w in range(2):
             hop1(w, t).wait_recv()
             hop2(w, t).start()
-    for w in range(2):
-        choose(1 + w, lambda t, spot: first_hop[w][t, spot])
-        spread(1 + w)
+        for w in range(2):
+            choose(1 + w, t, lambda spot: first_hop[w][t][spot])
+            spread(1 + w, t)
 
     each(1, LAYERS, lambda s: g2(s).wait_recv())
     total = g_col[0]
@@ -313,43 +339,49 @@
             table_copy(w, far).wait_recv()
     keep_tables.start()
     keep_tables.wait()
-    for w in range(2):
-        for t in range(2):
+    for t in range(2):
+        for w in range(2):
             hop2(w, t).wait_recv()
-        owner = col(-2 * ways[w])
-
-        def one(j, r, far):
-            spot = tables[2 * w + far - 1, mate(r), 0, owner]
-            for t in range(2):
-                pick3[w, j, pl.ds(t * BLOCK, BLOCK), :] = second_hop[w][t, spot]
-
-        each(0, 4, lambda j: one(j, 2 * j + w, 2))
-        each(0, PLANE, lambda r: one(4 + r, r, 1))
-        for c in range(5):
-            hop3(w, c).start()
-    for w in range(2):
-        choose(3 + w, lambda t, spot: second_hop[w][t, spot])
-        spread(3 + w)
-    for w in range(2):
-        hop3(w, 0).wait_recv()
-        hop4(w).start()
-    for c in range(1, 5):
-        for w in range(2):
-            hop3(w, c).wait_recv()
-            for r in (2 * c - 2, 2 * c - 1):
+            owner = col(-2 * ways[w])
+
+            def one(j, r, far):
+                pick3[w, t, j] = second_hop[w][t][tables[2 * w + far - 1, mate(r), 0, owner]]
+
+            each(0, 4, lambda j: one(j, 2 * j + w, 2))
+            hop3(w, t, 0).start()
+            each(0, PLANE, lambda r: one(4 + r, r, 1))
+            for c in (1, 2):
+                hop3(w, t, c).start()
+        for w in range(2):
+            choose(3 + w, t, lambda spot: second_hop[w][t][spot])
+            spread(3 + w, t)
+    for t in range(2):
+        for w in range(2):
+            hop3(w, t, 0).wait_recv()
+            hop4(w, t).start()
+        for c in (1, 2):
+            for w in range(2):
+                hop3(w, t, c).wait_recv()
+                for r in range(4 * c - 4, 4 * c):
+                    if r == 0:
+                        fetched[t, layer(5 + w) * PLANE + p_me] = got3[w, t, 4]
+                    else:
+                        spread_one(5 + w, t, r, got3.at[w, t, 4 + r]).start()
+        if t == 0:
+            for f in (1, 3, 2):
+                row_weight(f, lax.rem(row - f + 4, 4)).wait_recv()
+                core_weight(f, part_rows).start()
+            for w in range(2):
+                attend_layer(3 + w)
+    for t in range(2):
+        for w in range(2):
+            hop4(w, t).wait_recv()
+            for j in range(4):
+                r = 2 * j + w
                 if r == 0:
-                    fetched[layer(5 + w) * PLANE + p_me] = got3[w, 4]
+                    fetched[t, layer(7) * PLANE + p_me] = got4[w, t, j]
                 else:
-                    spread_one(5 + w, r, got3.at[w, 4 + r]).start()
-        if c <= 2:
-            attend_layer(2 + c)
-    for w in range(2):
-        hop4(w).wait_recv()
-    for r in range(PLANE):
-        if r == 0:
-            fetched[layer(7) * PLANE + p_me] = got4[0, 0]
-        else:
-            spread_one(7, r, got4.at[r % 2, r // 2]).start()
+                    spread_one(7, t, r, got4.at[w, t, j]).start()
     attend_layer(5)
     attend_layer(6)
     attend_layer(7)
@@ -394,15 +426,15 @@
         for w in range(2):
             hop1(w, t).wait_send()
             hop2(w, t).wait_send()
-    for w in range(2):
-        for c in range(5):
-            hop3(w, c).wait_send()
-        hop4(w).wait_send()
+            for c in range(3):
+                hop3(w, t, c).wait_send()
+            hop4(w, t).wait_send()
     for side in range(2):
         for t in range(2):
             halo_copy(side, t).wait_send()
     for d in range(LAYERS):
-        each(1, PLANE, lambda r: spread_one(d, r, fetched.at[0]).wait_send())
+        for t in range(2):
+            each(1, PLANE, lambda r: spread_one(d, t, r, fetched.at[t, 0]).wait_send())
     each(1, PLANE, lambda r: g1(r, mate(r)).wait_send())
     each(1, LAYERS, lambda s: g2(s).wait_send())
     each(1, PLANE, lambda r: g3(r, mate(r), p_me).wait_send())
@@ -411,13 +443,19 @@
     for w in range(2):
         for far in (1, 2):
             table_copy(w, far).wait_send()
+    own_weight.wait()
+    other_rows = pl.ds(pl.multiple_of((1 - core) * (depth // 2), depth // 2), depth // 2)
+    for f in range(1, 4):
+        row_weight(f, row).wait_send()
+        core_weight(f, part_rows).wait_send()
+        core_weight(f, other_rows).wait_recv()
     for f in range(1, 4):
         cross(context.at[quarter_at(0)], heads_ref.at[:, heads_at(row)], c_s.at[f], c_r.at[f], row).wait_send()
         came = lax.rem(row - f + 4, 4)
         cross(context.at[quarter_at(0)], heads_ref.at[:, heads_at(came)], c_s.at[f], c_r.at[f], row).wait_recv()
 
 
-def gather_attend(ids, shared_ids, query, keys, values):
+def gather_attend(ids, shared_ids, query, keys, values, weight):
     tokens, width = query.shape[0] * BLOCK, query.shape[2]
     n = PLANE * LAYERS
     pair = 2 * BLOCK
@@ -426,19 +464,22 @@
     vmem = pl.BlockSpec(memory_space=pltpu.VMEM)
     smem = pl.BlockSpec(memory_space=pltpu.SMEM)
     sem = pltpu.SemaphoreType.DMA
-    hop = pltpu.VMEM((2,) + query.shape, half)
+    hop = pltpu.VMEM(query.shape, half)
     return pl.pallas_call(
         kernel,
-        out_shape=jax.ShapeDtypeStruct((tokens // 4, 4 * width), half),
-        in_specs=[smem] * 2 + [vmem] * 3,
-        out_specs=vmem,
+        out_shape=[
+            jax.ShapeDtypeStruct((tokens // 4, 4 * width), half),
+            jax.ShapeDtypeStruct((4,) + weight.shape, half),
+        ],
+        in_specs=[smem] * 2 + [vmem] * 3 + [pl.BlockSpec(memory_space=pl.ANY)],
+        out_specs=[vmem, pl.BlockSpec(memory_space=pl.ANY)],
         scratch_shapes=[
-            pltpu.VMEM((n, pair, width), half),
-            hop, hop, hop, hop,
-            pltpu.VMEM((5, PLANE, pair, width), half),
-            pltpu.VMEM((2, 12, pair, width), half),
-            pltpu.VMEM((2, 12, pair, width), half),
-            pltpu.VMEM((2, 4, pair, width), half),
+            pltpu.VMEM((2, n, BLOCK, width), half),
+            hop, hop, hop, hop, hop, hop, hop, hop,
+            pltpu.VMEM((5, 2, PLANE, BLOCK, width), half),
+            pltpu.VMEM((2, 2, 12, BLOCK, width), half),
+            pltpu.VMEM((2, 2, 12, BLOCK, width), half),
+            pltpu.VMEM((2, 2, 4, BLOCK, width), half),
             pltpu.VMEM((2, pair, width), half),
             pltpu.VMEM((tokens + pair, width), half),
             pltpu.VMEM((tokens + pair, width), half),
@@ -463,24 +504,25 @@
             pltpu.SMEM((PLANE, PLANE, HD), jnp.int32),
             pltpu.SMEM((4, PLANE, PLANE, HD), jnp.int32),
             sem((2, 2)), sem((2, 2)), sem((2, 2)), sem((2, 2)),
-            sem((2, 5)), sem((2, 5)), sem((2,)), sem((2,)),
-            sem((LAYERS, PLANE)), sem((LAYERS, PLANE)),
+            sem((2, 2, 3)), sem((2, 2, 3)), sem((2, 2)), sem((2, 2)),
+            sem((2, LAYERS, PLANE)), sem((2, LAYERS, PLANE)),
             sem((2, 2)), sem((2, 2)), sem((3, 8)), sem((3, 8)), sem((4,)), sem((4,)),
-            sem((PLANE,)), sem((PLANE,)), sem((4,)), sem((4,)), sem((3,)),
+            sem((PLANE,)), sem((PLANE,)), sem((4,)), sem((4,)), sem((4,)),
+            sem((4,)), sem((4,)), sem((4,)), sem((4,)),
         ],
         compiler_params=pltpu.CompilerParams(
             collective_id=0, has_side_effects=True, vmem_limit_bytes=58 << 20
         ),
         cost_estimate=pl.CostEstimate(flops=3 * 10**9, bytes_accessed=10 * 10**6, transcendentals=4 * 10**6),
-    )(ids, shared_ids, query, keys, values)
+    )(ids, shared_ids, query, keys, values, weight)
 
 
 def on_device(query_rows, key_rows, value_rows, out_weight, random_ids, global_ids):
     tokens, width = query_rows.shape
     blocks = tokens // BLOCK
-    weight = lax.all_gather(out_weight, "fsdp", axis=0, tiled=True)
     rows = [array.reshape(blocks, BLOCK, width) for array in (query_rows, key_rows, value_rows)]
-    all_heads = gather_attend(random_ids, global_ids, *rows)
+    all_heads, weight = gather_attend(random_ids, global_ids, *rows, out_weight)
+    weight = weight.reshape(-1, out_weight.shape[1])
     return jnp.dot(all_heads, weight, preferred_element_type=jnp.float32).astype(jnp.bfloat16)
 
 

time: 221 us -> 202 us (0.914)
  between operations: 13.4 us -> 0.01 us
  Pallas kernels: 193 us -> 188 us
    pallas_call x1, Pallas kernels: 193 us -> 188 us  [gather_attend(): pl.pallas_call(kernel, out_shape=[jax.ShapeDtypeStruct((tokens // 4, 4 *...]
  transfers between devices with their start and end apart: 1 -> 0, of which waited for: 0 -> 0; matrix products, arithmetic and copies ran while one was open for 1% -> 0% of each run, Pallas kernels for 88% -> 0%
where the time goes in v4:
time: 202 us; the launch traced here: 201 us
  Pallas kernels  188 us (93%)
  matrix products  11.9 us (6%)
    pallas_call x1, Pallas kernels, gather_attend(): pl.pallas_call(kernel, out_shape=[jax.ShapeDtypeStruct((tokens // 4, 4 *...  188 us
    dot_general x1, matrix products, on_device(): jnp.dot(all_heads, weight, preferred_element_type=jnp.float32)  11.9 us

profile of v4, /device:TPU:1, one launch (start us, length us, event | category | flops | bytes accessed | tf_op | source)
XLA Modules:
  0.0 200.8 jit_solution(17559194629938243142)
XLA Ops:
  0.0 1.4 copy.7.ids
  1.4 187.5 %shard_map.64 = (bf16[256,2048]{1,0:T(8,128)(2,1)}, bf16[4,512,4096]{2,1,0:T(8,128)(2,1)}) custom-call(s32[16,3]{1,0:T(8,128)} %copy.7.ids, s32[2]{0:T(128)} %shared_ids.1, bf16[16,64,512]{2,1,0:T(8,128)(2,1)} %bitcast.6, bf16[16,64,512]{2,1,0:T(8,128)(2,1)} %bitcast.7, bf16[16,64,512]{2,1,0:T(8,128)(2,1)} %bitcast.8, bf16[512,4096]{1,0:T(8,128)(2,1)} %w_ref.1), custom_call_target="tpu_custom_call" | custom-call | flops 3000000000 | bytes 10000000 | tf_op jit(solution)/shard_map/pallas_call | solution.py:468
  188.9 11.9 %convolution_convert_fusion = bf16[256,4096]{1,0:T(8,128)(2,1)} fusion(bf16[256,2048]{1,0:T(8,128)(2,1)} %get-tuple-element.7, bf16[2048,4096]{1,0:T(8,128)(2,1)} %bitcast.9), kind=kOutput, calls=%fused_computation | convolution fusion | flops 4296015872 | bytes 19922944 | tf_op jit(solution)/shard_map/dot_general | solution.py:526

commit v5 on v4

--- a/solution.py
+++ b/solution.py
@@ -35,7 +35,7 @@
     halo, key_pad, value_pad, g_mine, g_in, g_part, g_col, g_sum, g_all,
     near_acc, near_max, near_sum, far_acc, far_max, far_sum, context,
     mine_v, inverse_v, table_v, tables_v, inverse, table, tables,
-    hop1_s, hop1_r, hop2_s, hop2_r, hop3_s, hop3_r, hop4_s, hop4_r,
+    hop1_s, hop1_r, hop2_s, hop2_r, hop3_s, hop3_r, hop4_s, hop4_r, relay_s, relay_r,
     in_s, in_r, halo_s, halo_r, g_s, g_r, c_s, c_r, t_s, t_r, far_s, far_r, local_s,
     row_s, row_r, core_s, core_r,
 ):
@@ -100,8 +100,20 @@
             pick3.at[w, t, part], got3.at[w, t, part], hop3_s.at[w, t, c], hop3_r.at[w, t, c], col(ways[w])
         )
 
-    def hop4(w, t):
-        return copy(got3.at[w, t, pl.ds(0, 4)], got4.at[w, t], hop4_s.at[w, t], hop4_r.at[w, t], col(ways[w]))
+    def relay(w, t, j):
+        return copy(
+            got3.at[w, t, j], got4.at[w, t, j], relay_s.at[w, t, j], relay_r.at[w, t, j],
+            z * PLANE + mate(2 * j + w),
+        )
+
+    def hop4(w, t, j):
+        src = got3.at[w, t, j] if 2 * j + w == 0 else got4.at[w, t, j]
+        owner = col(-3 * ways[w]) - p_me + from_mate(2 * j + w)
+        return copy(src, fetched.at[t, owner], hop4_s.at[w, t, j], hop4_r.at[w, t, j], col(ways[w]))
+
+    def last_arrived(w, t, j):
+        spot = fetched.at[t, layer(7) * PLANE + from_mate(2 * j + w)]
+        copy(spot, spot, hop4_s.at[w, t, j], hop4_r.at[w, t, j], col(ways[w])).wait_recv()
 
     core = lax.rem(me, 2)
     depth = w_ref.shape[0]
@@ -358,7 +370,8 @@
     for t in range(2):
         for w in range(2):
             hop3(w, t, 0).wait_recv()
-            hop4(w, t).start()
+            for j in range(4):
+                (hop4 if 2 * j + w == 0 else relay)(w, t, j).start()
         for c in (1, 2):
             for w in range(2):
                 hop3(w, t, c).wait_recv()
@@ -367,24 +380,25 @@
                         fetched[t, layer(5 + w) * PLANE + p_me] = got3[w, t, 4]
                     else:
                         spread_one(5 + w, t, r, got3.at[w, t, 4 + r]).start()
+            if c == 1:
+                for w in range(2):
+                    for j in range(4):
+                        if 2 * j + w > 0:
+                            relay(w, t, j).wait_recv()
+                            hop4(w, t, j).start()
         if t == 0:
             for f in (1, 3, 2):
                 row_weight(f, lax.rem(row - f + 4, 4)).wait_recv()
                 core_weight(f, part_rows).start()
             for w in range(2):
                 attend_layer(3 + w)
-    for t in range(2):
-        for w in range(2):
-            hop4(w, t).wait_recv()
-            for j in range(4):
-                r = 2 * j + w
-                if r == 0:
-                    fetched[t, layer(7) * PLANE + p_me] = got4[w, t, j]
-                else:
-                    spread_one(7, t, r, got4.at[w, t, j]).start()
     attend_layer(5)
     attend_layer(6)
-    attend_layer(7)
+    for w in range(2):
+        for j in range(4):
+            for t in range(2):
+                last_arrived(w, t, j)
+            attend(layer(7) * PLANE + from_mate(2 * j + w))
 
     quarter = tokens // 4
 
@@ -428,11 +442,14 @@
             hop2(w, t).wait_send()
             for c in range(3):
                 hop3(w, t, c).wait_send()
-            hop4(w, t).wait_send()
+            for j in range(4):
+                if 2 * j + w > 0:
+                    relay(w, t, j).wait_send()
+                hop4(w, t, j).wait_send()
     for side in range(2):
         for t in range(2):
             halo_copy(side, t).wait_send()
-    for d in range(LAYERS):
+    for d in range(LAYERS - 1):
         for t in range(2):
             each(1, PLANE, lambda r: spread_one(d, t, r, fetched.at[t, 0]).wait_send())
     each(1, PLANE, lambda r: g1(r, mate(r)).wait_send())
@@ -504,7 +521,7 @@
             pltpu.SMEM((PLANE, PLANE, HD), jnp.int32),
             pltpu.SMEM((4, PLANE, PLANE, HD), jnp.int32),
             sem((2, 2)), sem((2, 2)), sem((2, 2)), sem((2, 2)),
-            sem((2, 2, 3)), sem((2, 2, 3)), sem((2, 2)), sem((2, 2)),
+            sem((2, 2, 3)), sem((2, 2, 3)), sem((2, 2, 4)), sem((2, 2, 4)), sem((2, 2, 4)), sem((2, 2, 4)),
             sem((2, LAYERS, PLANE)), sem((2, LAYERS, PLANE)),
             sem((2, 2)), sem((2, 2)), sem((3, 8)), sem((3, 8)), sem((4,)), sem((4,)),
             sem((PLANE,)), sem((PLANE,)), sem((4,)), sem((4,)), sem((4,)),
@@ -517,13 +534,35 @@
     )(ids, shared_ids, query, keys, values, weight)
 
 
+def project_kernel(heads_ref, weight_ref, out_ref):
+    product = jnp.dot(heads_ref[...], weight_ref[...], preferred_element_type=jnp.float32)
+    out_ref[...] = product.astype(out_ref.dtype)
+
+
+def project(heads, weight):
+    rows, depth = heads.shape
+    columns = weight.shape[1]
+    tile = 512
+    return pl.pallas_call(
+        project_kernel,
+        grid=(columns // tile,),
+        in_specs=[
+            pl.BlockSpec((rows, depth), lambda i: (0, 0)),
+            pl.BlockSpec((depth, tile), lambda i: (0, i)),
+        ],
+        out_specs=pl.BlockSpec((rows, tile), lambda i: (0, i)),
+        out_shape=jax.ShapeDtypeStruct((rows, columns), heads.dtype),
+        compiler_params=pltpu.CompilerParams(vmem_limit_bytes=40 << 20),
+    )(heads, weight)
+
+
 def on_device(query_rows, key_rows, value_rows, out_weight, random_ids, global_ids):
     tokens, width = query_rows.shape
     blocks = tokens // BLOCK
     rows = [array.reshape(blocks, BLOCK, width) for array in (query_rows, key_rows, value_rows)]
     all_heads, weight = gather_attend(random_ids, global_ids, *rows, out_weight)
     weight = weight.reshape(-1, out_weight.shape[1])
-    return jnp.dot(all_heads, weight, preferred_element_type=jnp.float32).astype(jnp.bfloat16)
+    return project(all_heads, weight)
 
 
 def solution(mesh):

time: 202 us -> 199 us (0.985)
  matrix products: 11.9 us -> 0 us
  Pallas kernels: 188 us -> 196 us
    dot_general x1 -> x0, matrix products: 11.9 us -> none  [on_device(): jnp.dot(all_heads, weight, preferred_element_type=jnp.float32)]
    pallas_call x0 -> x1, Pallas kernels: none -> 11.4 us  [project(): pl.pallas_call(project_kernel, grid=(columns // tile,), in_specs=[pl.Bloc...]
    pallas_call x1, Pallas kernels: 188 us -> 185 us  [gather_attend(): pl.pallas_call(kernel, out_shape=[jax.ShapeDtypeStruct((tokens // 4, 4 *...]
where the time goes in v5:
time: 199 us
  Pallas kernels  196 us (98%)
  local copies, waits for them, and re-layouts  2.57 us (1%)
    pallas_call x1, Pallas kernels, gather_attend(): pl.pallas_call(kernel, out_shape=[jax.ShapeDtypeStruct((tokens // 4, 4 *...  185 us
    pallas_call x1, Pallas kernels, project(): pl.pallas_call(project_kernel, grid=(columns // tile,), in_specs=[pl.Bloc...  11.4 us

profile of v5, /device:TPU:1, one launch (start us, length us, event | category | flops | bytes accessed | tf_op | source)
XLA Modules:
  0.0 199.1 jit_solution(17214780206977791266)
XLA Ops:
  0.0 1.4 copy.7.ids
  1.4 185.1 %shard_map.64 = (bf16[256,2048]{1,0:T(8,128)(2,1)}, bf16[4,512,4096]{2,1,0:T(8,128)(2,1)}) custom-call(s32[16,3]{1,0:T(8,128)} %copy.7.ids, s32[2]{0:T(128)} %shared_ids.1, bf16[16,64,512]{2,1,0:T(8,128)(2,1)} %bitcast.5, bf16[16,64,512]{2,1,0:T(8,128)(2,1)} %bitcast.6, bf16[16,64,512]{2,1,0:T(8,128)(2,1)} %bitcast.7, bf16[512,4096]{1,0:T(8,128)(2,1)} %w_ref.1), custom_call_target="tpu_custom_call" | custom-call | flops 3000000000 | bytes 10000000 | tf_op jit(solution)/shard_map/pallas_call | solution.py:485
  186.4 0.0 copy-start
  186.4 1.2 copy-done
  187.7 11.4 %shard_map.65 = bf16[256,4096]{1,0:T(8,128)(2,1)} custom-call(bf16[256,2048]{1,0:T(8,128)(2,1)S(1)} %copy-done, bf16[2048,4096]{1,0:T(8,128)(2,1)} %bitcast.4), custom_call_target="tpu_custom_call" | custom-call | tf_op jit(solution)/shard_map/pallas_call | solution.py:546
Async XLA Ops:
  186.4 1.2 copy-start

commit v6 on v5

--- a/solution.py
+++ b/solution.py
@@ -29,15 +29,15 @@
 def kernel(
     ids, shared_ids,
     q_ref, k_ref, v_ref, w_ref,
-    heads_ref, weight_ref,
-    fetched,
+    out_ref, weight_ref,
+    result, heads_in, fetched,
     front1_k, front1_v, back1_k, back1_v, front2_k, front2_v, back2_k, back2_v, stage, pick3, got3, got4,
     halo, key_pad, value_pad, g_mine, g_in, g_part, g_col, g_sum, g_all,
     near_acc, near_max, near_sum, far_acc, far_max, far_sum, context,
     mine_v, inverse_v, table_v, tables_v, inverse, table, tables,
     hop1_s, hop1_r, hop2_s, hop2_r, hop3_s, hop3_r, hop4_s, hop4_r, relay_s, relay_r,
     in_s, in_r, halo_s, halo_r, g_s, g_r, c_s, c_r, t_s, t_r, far_s, far_r, local_s,
-    row_s, row_r, core_s, core_r,
+    row_s, row_r, core_s, core_r, load_s, out_s,
 ):
     me = lax.axis_index("seq")
     row = lax.axis_index("fsdp")
@@ -117,7 +117,7 @@
 
     core = lax.rem(me, 2)
     depth = w_ref.shape[0]
-    part_rows = pl.ds(pl.multiple_of(core * (depth // 2), depth // 2), depth // 2)
+    part_rows = pl.ds(core * (depth // 2), depth // 2)
 
     def row_weight(f, at):
         return cross(
@@ -130,14 +130,34 @@
             weight_ref.at[came, rows], weight_ref.at[came, rows], core_s.at[f], core_r.at[f], me + 1 - 2 * core
         )
 
-    own_weight = pltpu.make_async_copy(w_ref, weight_ref.at[row], local_s.at[3])
+    other_rows = pl.ds((1 - core) * (depth // 2), depth // 2)
+    chunk = 512
+    chunks = w_ref.shape[2] // chunk
+
+    def place(k, i):
+        if k < 2:
+            return (second_hop, first_hop)[k][i // 4][i // 2 % 2].at[pl.ds(depth * (i % 2), depth)]
+        if k == 2:
+            return stage.at[i // 2, i % 2]
+        return (pick3, got3)[i // 4].at[i // 2 % 2, i % 2, pl.ds(0, depth)]
+
+    def load(k, i):
+        columns_i = pl.ds(i * chunk, chunk)
+        if k == 0:
+            src = w_ref.at[:, :, columns_i]
+        else:
+            src = weight_ref.at[lax.rem(row - k + 4, 4), :, :, columns_i]
+        return pltpu.make_async_copy(src, place(k, i), load_s.at[k, i])
+
+    def load_all(k):
+        for i in range(chunks):
+            load(k, i).start()
 
     for t in range(2):
         for w in range(2):
             hop1(w, t).start()
     for f in (1, 3, 2):
         row_weight(f, row).start()
-    own_weight.start()
 
     def halo_copy(side, t):
         block = tokens // BLOCK - 1 if side == 0 else 0
@@ -392,8 +412,19 @@
                 core_weight(f, part_rows).start()
             for w in range(2):
                 attend_layer(3 + w)
+            load_all(0)
     attend_layer(5)
     attend_layer(6)
+    for w in range(2):
+        for t in range(2):
+            hop2(w, t).wait_send()
+    for f in range(1, 4):
+        core_weight(f, other_rows).wait_recv()
+    load_all(1)
+    for d in range(5):
+        for t in range(2):
+            each(1, PLANE, lambda r: spread_one(d, t, r, fetched.at[t, 0]).wait_send())
+    load_all(2)
     for w in range(2):
         for j in range(4):
             for t in range(2):
@@ -424,34 +455,65 @@
     def quarter_at(f):
         return pl.ds(pl.multiple_of(f * quarter, quarter), quarter)
 
-    def heads_at(f):
-        return pl.ds(pl.multiple_of(f * width, width), width)
+    def exchange(f):
+        to = lax.rem(row + f, 4)
+        return cross(context.at[quarter_at(to)], heads_in.at[f], c_s.at[f], c_r.at[f], to)
+
+    for t in range(2):
+        for w in range(2):
+            for c in range(3):
+                hop3(w, t, c).wait_send()
+            for j in range(4):
+                if 2 * j + w > 0:
+                    relay(w, t, j).wait_send()
+                else:
+                    hop4(w, t, j).wait_send()
+            each(1, PLANE, lambda r: spread_one(5 + w, t, r, fetched.at[t, 0]).wait_send())
+    load_all(3)
 
     blocks = quarter // BLOCK
     for f in (2, 1, 3, 0):
         to = lax.rem(row + f, 4)
         each(0, blocks, lambda b: merge(to * blocks + b))
         if f > 0:
-            cross(context.at[quarter_at(to)], heads_ref.at[:, heads_at(row)], c_s.at[f], c_r.at[f], to).start()
-        else:
-            heads_ref[:, heads_at(row)] = context[quarter_at(row), :]
+            exchange(f).start()
+
+    def tile_of(k, i):
+        return place(k, i)[...].reshape(depth * BLOCK, chunk)
+
+    group = quarter // BLOCK
+
+    def product(block, k, i):
+        return jnp.dot(block, tile_of(k, i), preferred_element_type=jnp.float32)
+
+    mine = context[quarter_at(row), :]
+    for i in range(chunks):
+        load(0, i).wait()
+        far_acc[pl.ds(group * i, group)] = product(mine, 0, i).reshape(group, BLOCK, chunk)
+    for f in (2, 1, 3):
+        exchange(f).wait_recv()
+
+    def write(i):
+        columns_i = pl.ds(i * chunk, chunk)
+        return pltpu.make_async_copy(result.at[:, columns_i], out_ref.at[:, columns_i], out_s.at[i])
+
+    for i in range(chunks):
+        part = far_acc[pl.ds(group * i, group)].reshape(quarter, chunk)
+        for f in (1, 2, 3):
+            load(f, i).wait()
+            part = part + product(heads_in[f], f, i)
+        result[:, pl.ds(i * chunk, chunk)] = part.astype(jnp.bfloat16)
+        write(i).start()
 
     for t in range(2):
         for w in range(2):
             hop1(w, t).wait_send()
-            hop2(w, t).wait_send()
-            for c in range(3):
-                hop3(w, t, c).wait_send()
             for j in range(4):
                 if 2 * j + w > 0:
-                    relay(w, t, j).wait_send()
-                hop4(w, t, j).wait_send()
+                    hop4(w, t, j).wait_send()
     for side in range(2):
         for t in range(2):
             halo_copy(side, t).wait_send()
-    for d in range(LAYERS - 1):
-        for t in range(2):
-            each(1, PLANE, lambda r: spread_one(d, t, r, fetched.at[t, 0]).wait_send())
     each(1, PLANE, lambda r: g1(r, mate(r)).wait_send())
     each(1, LAYERS, lambda s: g2(s).wait_send())
     each(1, PLANE, lambda r: g3(r, mate(r), p_me).wait_send())
@@ -460,16 +522,12 @@
     for w in range(2):
         for far in (1, 2):
             table_copy(w, far).wait_send()
-    own_weight.wait()
-    other_rows = pl.ds(pl.multiple_of((1 - core) * (depth // 2), depth // 2), depth // 2)
     for f in range(1, 4):
         row_weight(f, row).wait_send()
         core_weight(f, part_rows).wait_send()
-        core_weight(f, other_rows).wait_recv()
-    for f in range(1, 4):
-        cross(context.at[quarter_at(0)], heads_ref.at[:, heads_at(row)], c_s.at[f], c_r.at[f], row).wait_send()
-        came = lax.rem(row - f + 4, 4)
-        cross(context.at[quarter_at(0)], heads_ref.at[:, heads_at(came)], c_s.at[f], c_r.at[f], row).wait_recv()
+        exchange(f).wait_send()
+    for i in range(chunks):
+        write(i).wait()
 
 
 def gather_attend(ids, shared_ids, query, keys, values, weight):
@@ -485,12 +543,14 @@
     return pl.pallas_call(
         kernel,
         out_shape=[
-            jax.ShapeDtypeStruct((tokens // 4, 4 * width), half),
+            jax.ShapeDtypeStruct((tokens // 4, weight.shape[2]), half),
             jax.ShapeDtypeStruct((4,) + weight.shape, half),
         ],
         in_specs=[smem] * 2 + [vmem] * 3 + [pl.BlockSpec(memory_space=pl.ANY)],
-        out_specs=[vmem, pl.BlockSpec(memory_space=pl.ANY)],
+        out_specs=[pl.BlockSpec(memory_space=pl.ANY)] * 2,
         scratch_shapes=[
+            pltpu.VMEM((tokens // 4, weight.shape[2]), half),
+            pltpu.VMEM((4, tokens // 4, width), half),
             pltpu.VMEM((2, n, BLOCK, width), half),
             hop, hop, hop, hop, hop, hop, hop, hop,
             pltpu.VMEM((5, 2, PLANE, BLOCK, width), half),
@@ -524,8 +584,8 @@
             sem((2, 2, 3)), sem((2, 2, 3)), sem((2, 2, 4)), sem((2, 2, 4)), sem((2, 2, 4)), sem((2, 2, 4)),
             sem((2, LAYERS, PLANE)), sem((2, LAYERS, PLANE)),
             sem((2, 2)), sem((2, 2)), sem((3, 8)), sem((3, 8)), sem((4,)), sem((4,)),
-            sem((PLANE,)), sem((PLANE,)), sem((4,)), sem((4,)), sem((4,)),
-            sem((4,)), sem((4,)), sem((4,)), sem((4,)),
+            sem((PLANE,)), sem((PLANE,)), sem((4,)), sem((4,)), sem((3,)),
+            sem((4,)), sem((4,)), sem((4,)), sem((4,)), sem((4, 8)), sem((8,)),
         ],
         compiler_params=pltpu.CompilerParams(
             collective_id=0, has_side_effects=True, vmem_limit_bytes=58 << 20
@@ -534,35 +594,12 @@
     )(ids, shared_ids, query, keys, values, weight)
 
 
-def project_kernel(heads_ref, weight_ref, out_ref):
-    product = jnp.dot(heads_ref[...], weight_ref[...], preferred_element_type=jnp.float32)
-    out_ref[...] = product.astype(out_ref.dtype)
-
-
-def project(heads, weight):
-    rows, depth = heads.shape
-    columns = weight.shape[1]
-    tile = 512
-    return pl.pallas_call(
-        project_kernel,
-        grid=(columns // tile,),
-        in_specs=[
-            pl.BlockSpec((rows, depth), lambda i: (0, 0)),
-            pl.BlockSpec((depth, tile), lambda i: (0, i)),
-        ],
-        out_specs=pl.BlockSpec((rows, tile), lambda i: (0, i)),
-        out_shape=jax.ShapeDtypeStruct((rows, columns), heads.dtype),
-        compiler_params=pltpu.CompilerParams(vmem_limit_bytes=40 << 20),
-    )(heads, weight)
-
-
 def on_device(query_rows, key_rows, value_rows, out_weight, random_ids, global_ids):
     tokens, width = query_rows.shape
     blocks = tokens // BLOCK
     rows = [array.reshape(blocks, BLOCK, width) for array in (query_rows, key_rows, value_rows)]
-    all_heads, weight = gather_attend(random_ids, global_ids, *rows, out_weight)
-    weight = weight.reshape(-1, out_weight.shape[1])
-    return project(all_heads, weight)
+    weight = out_weight.reshape(-1, BLOCK, out_weight.shape[1])
+    return gather_attend(random_ids, global_ids, *rows, weight)[0]
 
 
 def solution(mesh):

time: 199 us -> 196 us (0.985)
  Pallas kernels: 196 us -> 192 us
    pallas_call x2 -> x1, Pallas kernels: 196 us -> 192 us  [gather_attend(): pl.pallas_call(kernel, out_shape=[jax.ShapeDtypeStruct((tokens // 4, weig...]
    unnamed x3 -> x2, local copies, waits for them, and re-layouts: 2.57 us -> 4.48 us
where the time goes in v6:
time: 196 us
  Pallas kernels  192 us (98%)
  local copies, waits for them, and re-layouts  4.48 us (2%)
    pallas_call x1, Pallas kernels, gather_attend(): pl.pallas_call(kernel, out_shape=[jax.ShapeDtypeStruct((tokens // 4, weig...  192 us
    unnamed x2, local copies, waits for them, and re-layouts  4.48 us

profile of v6, /device:TPU:1, one launch (start us, length us, event | category | flops | bytes accessed | tf_op | source)
XLA Modules:
  0.0 196.1 jit_solution(2141806383592487706)
XLA Ops:
  0.0 1.4 copy.7.ids
  1.4 191.6 %shard_map.64 = (bf16[256,4096]{1,0:T(8,128)(2,1)}, bf16[4,8,64,4096]{3,2,1,0:T(8,128)(2,1)}) custom-call(s32[16,3]{1,0:T(8,128)} %copy.7.ids, s32[2]{0:T(128)} %shared_ids.1, bf16[16,64,512]{2,1,0:T(8,128)(2,1)} %bitcast.5, bf16[16,64,512]{2,1,0:T(8,128)(2,1)} %bitcast.6, bf16[16,64,512]{2,1,0:T(8,128)(2,1)} %bitcast.7, bf16[8,64,4096]{2,1,0:T(8,128)(2,1)} %bitcast.4), custom_call_target="tpu_custom_call" | custom-call | flops 3000000000 | bytes 10000000 | tf_op jit(solution)/shard_map/pallas_call | solution.py:543
  193.0 3.1 %copy.9 = bf16[256,4096]{1,0:T(8,128)(2,1)} copy(bf16[256,4096]{1,0:T(8,128)(2,1)} %get-tuple-element.6) | data formatting | bytes 4194304

commit v7 on v6

--- a/solution.py
+++ b/solution.py
@@ -459,6 +459,16 @@
         to = lax.rem(row + f, 4)
         return cross(context.at[quarter_at(to)], heads_in.at[f], c_s.at[f], c_r.at[f], to)
 
+    blocks = quarter // BLOCK
+    for f in (2, 1, 3, 0):
+        to = lax.rem(row + f, 4)
+        each(0, blocks, lambda b: merge(to * blocks + b))
+        if f > 0:
+            exchange(f).start()
+
+    def tile_of(k, i):
+        return place(k, i)[...].reshape(depth * BLOCK, chunk)
+
     for t in range(2):
         for w in range(2):
             for c in range(3):
@@ -470,16 +480,6 @@
                     hop4(w, t, j).wait_send()
             each(1, PLANE, lambda r: spread_one(5 + w, t, r, fetched.at[t, 0]).wait_send())
     load_all(3)
-
-    blocks = quarter // BLOCK
-    for f in (2, 1, 3, 0):
-        to = lax.rem(row + f, 4)
-        each(0, blocks, lambda b: merge(to * blocks + b))
-        if f > 0:
-            exchange(f).start()
-
-    def tile_of(k, i):
-        return place(k, i)[...].reshape(depth * BLOCK, chunk)
 
     group = quarter // BLOCK
 

time: 196 us -> 196 us (level)
  no operation moved by 1% of the time
where the time goes in v7:
time: 196 us
  Pallas kernels  191 us (97%)
  local copies, waits for them, and re-layouts  4.48 us (2%)
    pallas_call x1, Pallas kernels, gather_attend(): pl.pallas_call(kernel, out_shape=[jax.ShapeDtypeStruct((tokens // 4, weig...  191 us
    unnamed x2, local copies, waits for them, and re-layouts  4.48 us

profile of v7, /device:TPU:1, one launch (start us, length us, event | category | flops | bytes accessed | tf_op | source)
XLA Modules:
  0.0 195.9 jit_solution(5177833251483225875)
XLA Ops:
  0.0 1.4 copy.7.ids
  1.4 191.4 %shard_map.64 = (bf16[256,4096]{1,0:T(8,128)(2,1)}, bf16[4,8,64,4096]{3,2,1,0:T(8,128)(2,1)}) custom-call(s32[16,3]{1,0:T(8,128)} %copy.7.ids, s32[2]{0:T(128)} %shared_ids.1, bf16[16,64,512]{2,1,0:T(8,128)(2,1)} %bitcast.5, bf16[16,64,512]{2,1,0:T(8,128)(2,1)} %bitcast.6, bf16[16,64,512]{2,1,0:T(8,128)(2,1)} %bitcast.7, bf16[8,64,4096]{2,1,0:T(8,128)(2,1)} %bitcast.4), custom_call_target="tpu_custom_call" | custom-call | flops 3000000000 | bytes 10000000 | tf_op jit(solution)/shard_map/pallas_call | solution.py:543
  192.8 3.1 %copy.9 = bf16[256,4096]{1,0:T(8,128)(2,1)} copy(bf16[256,4096]{1,0:T(8,128)(2,1)} %get-tuple-element.6) | data formatting | bytes 4194304
